TPU v7x, 256 devices: a whole 4x4x8 slice. The times are simulated.
256 devices in a mesh: replica: 32 (over x_lo, z, core), tensor: 8 (over x_hi, y).
Axes of the slice: x: 4 (x_hi: 2, x_lo: 2; x = x_hi * 2 + x_lo), y: 4, z: 8, core: 2. Of those that a mesh axis runs over, the one named last changes fastest.
Arguments:
- context: bfloat16 [32, 2048, 1792], P('replica', None, 'tensor'), may hold values from -6 to 6
- out_grad: bfloat16 [32, 2048, 3584], P('replica', 'tensor'), may hold values from -6 to 6
- params: float32 [32, 1792, 3584], P('replica', 'tensor'), may hold values from -6 to 6
- momentum: bfloat16 [32, 1792, 3584], P('replica', 'tensor'), may hold values from -180 to 180
Outputs:
- mixed_params: float32 [32, 1792, 3584], P('replica', 'tensor')
- mixed_momentum: bfloat16 [32, 1792, 3584], P('replica', 'tensor')
All inputs are finite; a program needn't handle non-finite values.
Results may differ from a plain program's by a relative error of at most 0.0052.
Values may be sent and summed in bfloat16 or wider, within the bound.
No kernel may reach another device: no remote copies, remote signals or barrier semaphores. Data moves between devices by JAX's collectives and lax.ppermute only.
A program may use at most 128 MiB of HBM per device.

v0:
```python
import jax
import jax.numpy as jnp
from jax import lax
from jax.sharding import PartitionSpec as P

learn_rate = 0.01
beta_decay = 0.9


def passed_along(value, axis, steps):
    count = lax.axis_size(axis)
    pairs = [(source, (source + steps) % count) for source in range(count)]
    return lax.ppermute(value, axis, pairs)


def blend(own, below, above):
    return (own + below.astype(jnp.float32) + above.astype(jnp.float32)) / 3.0


def body(context, out_grad, params, momentum):
    local_ctx = context[0]
    gathered = lax.all_gather(out_grad, "tensor", axis=1, tiled=True)
    grad = lax.dot_general(
        local_ctx, gathered[0], (((0,), (0,)), ((), ())), preferred_element_type=jnp.float32
    )
    velocity = beta_decay * momentum[0].astype(jnp.float32) + grad
    stepped = params[0] - learn_rate * velocity
    step_sent = stepped.astype(jnp.bfloat16)
    vel_sent = velocity.astype(jnp.bfloat16)
    lower_one = passed_along((step_sent, vel_sent), "replica", 1)
    upper_one = passed_along((step_sent, vel_sent), "replica", -1)
    params_one = blend(stepped, lower_one[0], upper_one[0])
    velocity_one = blend(velocity, lower_one[1], upper_one[1])
    param_sent = params_one.astype(jnp.bfloat16)
    speed_sent = velocity_one.astype(jnp.bfloat16)
    lower_two = passed_along((param_sent, speed_sent), "replica", 2)
    upper_two = passed_along((param_sent, speed_sent), "replica", -2)
    params_two = blend(params_one, lower_two[0], upper_two[0])
    velocity_two = blend(velocity_one, lower_two[1], upper_two[1])
    return (params_two[None], velocity_two.astype(jnp.bfloat16)[None])


def solution(mesh):
    return jax.shard_map(
        body,
        mesh=mesh,
        in_specs=(
            P("replica", None, "tensor"),
            P("replica", "tensor", None),
            P("replica", "tensor", None),
            P("replica", "tensor", None),
        ),
        out_specs=(P("replica", "tensor", None), P("replica", "tensor", None)),
        check_vma=False,
    )
```

profile of v0, /device:TPU:1, one launch (start us, length us, event | category | flops | bytes accessed | tf_op | source)
XLA Modules:
  0.0 320.8 jit_solution(2887409313065282749)
XLA Ops:
  7.2 0.0 copy-start
  7.2 0.0 all-gather.2.cloned.1.call-start
  7.2 0.7 all-gather.2.cloned.1.call-update
  7.9 175.0 %all-gather.2.cloned.1.call-done = bf16[1,2048,3584]{2,1,0:T(8,128)(2,1)} async-done(((bf16[1,256,3584]{2,1,0:T(8,128)(2,1)}), bf16[1,2048,3584]{2,1,0:T(8,128)(2,1)}) %all-gather.2.cloned.1.call-update) | async-done | bytes 14680080 | tf_op jit(solution)/shard_map/all_gather | solution.py:22
  182.9 0.0 copy-done
  182.9 0.0 copy-start.1
  182.9 10.3 %fusion.10 = (bf16[224,3584]{1,0:T(8,128)(2,1)S(1)}, bf16[224,3584]{1,0:T(8,128)(2,1)S(1)}, f32[224,3584]{1,0:T(8,128)S(1)}) fusion(f32[1,224,3584]{2,1,0:T(8,128)} %param.6, bf16[1,2048,3584]{2,1,0:T(8,128)(2,1)} %all-gather.2.cloned.1.call-done, bf16[1,2048,224]{1,2,0:T(8,128)(2,1)S(1)} %copy-done, bf16[1,224,3584]{2,1,0:T(8,128)(2,1)} %param.7), kind=kOutput, calls=%fused_computation.13 | convolution fusion | flops 3293954048 | bytes 26836992 | tf_op jit(solution)/shard_map/dot_general | solution.py:23
  193.3 1.2 collective-permute-start.5
  194.4 1.2 collective-permute-start.4
  195.7 1.1 collective-permute-start.1
  196.8 0.6 collective-permute-start
  197.4 16.9 %collective-permute-done.5 = bf16[224,3584]{1,0:T(8,128)(2,1)S(1)} collective-permute-done((bf16[224,3584]{1,0:T(8,128)(2,1)S(1)}, bf16[224,3584]{1,0:T(8,128)(2,1)S(1)}, u32[]{:S(2)}, u32[]{:S(2)}) %collective-permute-start.5) | collective-permute-done | bytes 1605664 | tf_op jit(solution)/shard_map/ppermute | solution.py:13
  214.4 0.0 collective-permute-done.4
  214.4 17.2 %collective-permute-done.1 = bf16[224,3584]{1,0:T(8,128)(2,1)S(1)} collective-permute-done((bf16[224,3584]{1,0:T(8,128)(2,1)S(1)}, bf16[224,3584]{1,0:T(8,128)(2,1)S(1)}, u32[]{:S(2)}, u32[]{:S(2)}) %collective-permute-start.1) | collective-permute-done | bytes 1605664 | tf_op jit(solution)/shard_map/ppermute | solution.py:13
  231.6 0.0 collective-permute-done
  231.6 0.0 copy-done.1
  231.6 1.4 fusion.7
  233.0 4.4 %collective-permute-start.7 = (bf16[224,3584]{1,0:T(8,128)(2,1)S(1)}, bf16[224,3584]{1,0:T(8,128)(2,1)S(1)}, u32[]{:S(2)}, u32[]{:S(2)}) collective-permute-start(bf16[224,3584]{1,0:T(8,128)(2,1)S(1)} %get-tuple-element.4), channel_id=1, source_target_pairs={{0,240},{8,248},{16,0},{24,8},{32,16},{40,24},{48,32},{56,40},{64,... | collective-permute-start | bytes 4816904 | tf_op jit(solution)/shard_map/ppermute | solution.py:13
  237.4 0.0 collective-permute-start.6
  237.5 3.6 %collective-permute-start.3 = (bf16[224,3584]{1,0:T(8,128)(2,1)S(1)}, bf16[224,3584]{1,0:T(8,128)(2,1)S(1)}, u32[]{:S(2)}, u32[]{:S(2)}) collective-permute-start(bf16[224,3584]{1,0:T(8,128)(2,1)S(1)} %get-tuple-element.5), channel_id=1, source_target_pairs={{0,240},{8,248},{16,0},{24,8},{32,16},{40,24},{48,32},{56,40},{64,... | collective-permute-start | bytes 4816904 | tf_op jit(solution)/shard_map/ppermute | solution.py:13
  241.0 0.0 collective-permute-start.2
  241.0 30.8 %collective-permute-done.7 = bf16[224,3584]{1,0:T(8,128)(2,1)S(1)} collective-permute-done((bf16[224,3584]{1,0:T(8,128)(2,1)S(1)}, bf16[224,3584]{1,0:T(8,128)(2,1)S(1)}, u32[]{:S(2)}, u32[]{:S(2)}) %collective-permute-start.7) | collective-permute-done | bytes 1605664 | tf_op jit(solution)/shard_map/ppermute | solution.py:13
  271.8 3.9 %collective-permute-done.6 = bf16[224,3584]{1,0:T(8,128)(2,1)S(1)} collective-permute-done((bf16[224,3584]{1,0:T(8,128)(2,1)S(1)}, bf16[224,3584]{1,0:T(8,128)(2,1)S(1)}, u32[]{:S(2)}, u32[]{:S(2)}) %collective-permute-start.6) | collective-permute-done | bytes 1605664 | tf_op jit(solution)/shard_map/ppermute | solution.py:13
  275.7 30.5 %collective-permute-done.3 = bf16[224,3584]{1,0:T(8,128)(2,1)S(1)} collective-permute-done((bf16[224,3584]{1,0:T(8,128)(2,1)S(1)}, bf16[224,3584]{1,0:T(8,128)(2,1)S(1)}, u32[]{:S(2)}, u32[]{:S(2)}) %collective-permute-start.3) | collective-permute-done | bytes 1605664 | tf_op jit(solution)/shard_map/ppermute | solution.py:13
  306.3 3.9 %collective-permute-done.2 = bf16[224,3584]{1,0:T(8,128)(2,1)S(1)} collective-permute-done((bf16[224,3584]{1,0:T(8,128)(2,1)S(1)}, bf16[224,3584]{1,0:T(8,128)(2,1)S(1)}, u32[]{:S(2)}, u32[]{:S(2)}) %collective-permute-start.2) | collective-permute-done | bytes 1605664 | tf_op jit(solution)/shard_map/ppermute | solution.py:13
  310.1 3.8 %fusion.5 = (bf16[1,224,3584]{2,1,0:T(8,128)(2,1)}, f32[1,224,3584]{2,1,0:T(8,128)}) fusion(bf16[224,3584]{1,0:T(8,128)(2,1)S(1)} %collective-permute-done.7, bf16[224,3584]{1,0:T(8,128)(2,1)S(1)} %collective-permute-done.6, bf16[224,3584]{1,0:T(8,128)(2,1)S(1)} %collective-permute-done.5, f32[224,3584]{1,0:T(8,128)S(1)} %get-tuple-element.8, ...), kind=kLoop, calls=%fused_computation.8 | loop fusion | flops 18464768 | bytes 24084480 | tf_op jit(solution)/shard_map/broadcast_in_dim | solution.py:40
Async XLA Ops:
  7.2 175.8 %copy-start = (bf16[1,2048,224]{1,2,0:T(8,128)(2,1)S(1)}, bf16[1,2048,224]{1,2,0:T(8,128)(2,1)}, u32[]{:S(2)}) copy-start(bf16[1,2048,224]{1,2,0:T(8,128)(2,1)} %param.4) | copy-start | bytes 2752516
  7.2 175.8 %all-gather.2.cloned.1.call-start = ((), (), s32[]{:S(2)}) async-start(), calls=%async_computation | async-start | bytes 16515072 | tf_op jit(solution)/shard_map/all_gather | solution.py:22
  182.9 48.6 %copy-start.1 = (f32[1,224,3584]{2,1,0:T(8,128)S(1)}, f32[1,224,3584]{2,1,0:T(8,128)}, u32[]{:S(2)}) copy-start(f32[1,224,3584]{2,1,0:T(8,128)} %param.6) | copy-start | bytes 9633796
  193.3 21.1 %collective-permute-start.5 = (bf16[224,3584]{1,0:T(8,128)(2,1)S(1)}, bf16[224,3584]{1,0:T(8,128)(2,1)S(1)}, u32[]{:S(2)}, u32[]{:S(2)}) collective-permute-start(bf16[224,3584]{1,0:T(8,128)(2,1)S(1)} %get-tuple-element.6), channel_id=1, source_target_pairs={{0,248},{8,0},{16,8},{24,16},{32,24},{40,32},{48,40},{56,48},{64,5... | collective-permute-start | bytes 4816904 | tf_op jit(solution)/shard_map/ppermute | solution.py:13
  194.4 19.9 %collective-permute-start.4 = (bf16[224,3584]{1,0:T(8,128)(2,1)S(1)}, bf16[224,3584]{1,0:T(8,128)(2,1)S(1)}, u32[]{:S(2)}, u32[]{:S(2)}) collective-permute-start(bf16[224,3584]{1,0:T(8,128)(2,1)S(1)} %get-tuple-element.6), channel_id=1, source_target_pairs={{0,8},{8,16},{16,24},{24,32},{32,40},{40,48},{48,56},{56,64},{64,7... | collective-permute-start | bytes 4816904 | tf_op jit(solution)/shard_map/ppermute | solution.py:13
  195.7 35.9 %collective-permute-start.1 = (bf16[224,3584]{1,0:T(8,128)(2,1)S(1)}, bf16[224,3584]{1,0:T(8,128)(2,1)S(1)}, u32[]{:S(2)}, u32[]{:S(2)}) collective-permute-start(bf16[224,3584]{1,0:T(8,128)(2,1)S(1)} %get-tuple-element.7), channel_id=1, source_target_pairs={{0,248},{8,0},{16,8},{24,16},{32,24},{40,32},{48,40},{56,48},{64,5... | collective-permute-start | bytes 4816904 | tf_op jit(solution)/shard_map/ppermute | solution.py:13
  196.8 34.8 %collective-permute-start = (bf16[224,3584]{1,0:T(8,128)(2,1)S(1)}, bf16[224,3584]{1,0:T(8,128)(2,1)S(1)}, u32[]{:S(2)}, u32[]{:S(2)}) collective-permute-start(bf16[224,3584]{1,0:T(8,128)(2,1)S(1)} %get-tuple-element.7), channel_id=1, source_target_pairs={{0,8},{8,16},{16,24},{24,32},{32,40},{40,48},{48,56},{56,64},{64,7... | collective-permute-start | bytes 4816904 | tf_op jit(solution)/shard_map/ppermute | solution.py:13
  233.0 38.8 %collective-permute-start.7 = (bf16[224,3584]{1,0:T(8,128)(2,1)S(1)}, bf16[224,3584]{1,0:T(8,128)(2,1)S(1)}, u32[]{:S(2)}, u32[]{:S(2)}) collective-permute-start(bf16[224,3584]{1,0:T(8,128)(2,1)S(1)} %get-tuple-element.4), channel_id=1, source_target_pairs={{0,240},{8,248},{16,0},{24,8},{32,16},{40,24},{48,32},{56,40},{64,... | collective-permute-start | bytes 4816904 | tf_op jit(solution)/shard_map/ppermute | solution.py:13
  237.4 38.3 %collective-permute-start.6 = (bf16[224,3584]{1,0:T(8,128)(2,1)S(1)}, bf16[224,3584]{1,0:T(8,128)(2,1)S(1)}, u32[]{:S(2)}, u32[]{:S(2)}) collective-permute-start(bf16[224,3584]{1,0:T(8,128)(2,1)S(1)} %get-tuple-element.4), channel_id=1, source_target_pairs={{0,16},{8,24},{16,32},{24,40},{32,48},{40,56},{48,64},{56,72},{64,... | collective-permute-start | bytes 4816904 | tf_op jit(solution)/shard_map/ppermute | solution.py:13
  237.5 68.8 %collective-permute-start.3 = (bf16[224,3584]{1,0:T(8,128)(2,1)S(1)}, bf16[224,3584]{1,0:T(8,128)(2,1)S(1)}, u32[]{:S(2)}, u32[]{:S(2)}) collective-permute-start(bf16[224,3584]{1,0:T(8,128)(2,1)S(1)} %get-tuple-element.5), channel_id=1, source_target_pairs={{0,240},{8,248},{16,0},{24,8},{32,16},{40,24},{48,32},{56,40},{64,... | collective-permute-start | bytes 4816904 | tf_op jit(solution)/shard_map/ppermute | solution.py:13
  241.0 69.1 %collective-permute-start.2 = (bf16[224,3584]{1,0:T(8,128)(2,1)S(1)}, bf16[224,3584]{1,0:T(8,128)(2,1)S(1)}, u32[]{:S(2)}, u32[]{:S(2)}) collective-permute-start(bf16[224,3584]{1,0:T(8,128)(2,1)S(1)} %get-tuple-element.5), channel_id=1, source_target_pairs={{0,16},{8,24},{16,32},{24,40},{32,48},{40,56},{48,64},{56,72},{64,... | collective-permute-start | bytes 4816904 | tf_op jit(solution)/shard_map/ppermute | solution.py:13
Sparse Core Ops, SparseCore 0:
  10.6 172.2 all-gather.1
where the time goes:
time: 321 us
  waiting for transfers between devices  279 us (87%)
  between operations  14.1 us (4%)
  starting transfers between devices  12.2 us (4%)
  matrix products  10.3 us (3%)
  other arithmetic  5.22 us (2%)
    all_gather x1, waiting for transfers between devices, body(): gathered = lax.all_gather(out_grad, 'tensor', axis=1, tiled=True)  175 us
    ppermute x8, waiting for transfers between devices, passed_along(): return lax.ppermute(value, axis, pairs)  103 us
    ppermute x8, starting transfers between devices, passed_along(): return lax.ppermute(value, axis, pairs)  12.2 us
    dot_general x1, matrix products, body(): lax.dot_general(local_ctx, gathered[0], (((0,), (0,)), ((), ())), preferr...  10.3 us
  transfers between devices with their start and end apart: 9, of which 7 were waited for; matrix products, arithmetic and copies ran while one was open for 0% of the time, Pallas kernels for 0%

commit v1 on v0

v1 whole, which is shorter than its diff:
```python
import functools

import jax
import jax.numpy as jnp
from jax import lax
from jax.experimental import pallas as pl
from jax.experimental.pallas import tpu as pltpu
from jax.sharding import PartitionSpec as P

learn_rate = 0.01
beta_decay = 0.9

BOTH = ("replica", "tensor")
TILE = 256
CHUNKS = ((0, 4), (4, 3))
HALF_TILES = 7
bf16, f32 = jnp.bfloat16, jnp.float32


def passed_along(value, axis, steps):
    count = lax.axis_size(axis)
    pairs = [(source, (source + steps) % count) for source in range(count)]
    return lax.ppermute(value, axis, pairs)


def swap_half(value):
    return lax.ppermute(value, "tensor", [(t, t ^ 4) for t in range(8)])


def ring_step(value):
    pairs = []
    for r in range(32):
        way = 1 if r % 2 == 0 else -1
        for t in range(8):
            pairs.append((r * 8 + t, r * 8 + (t & 4) + ((t + way) & 3)))
    return lax.ppermute(value, BOTH, pairs)


def grad_kernel(s_ref, own_ref, oth_ref, g0, g1, g2, g3, mom_ref, v32_ref, v16_ref, goth_ref):
    acc_own = jnp.zeros(goth_ref.shape, f32)
    acc_oth = jnp.zeros(goth_ref.shape, f32)
    for step, blocks in enumerate((g0, g1, g2, g3)):
        for part in range(2):
            tokens = pl.ds(pl.multiple_of(s_ref[1 + 2 * step + part] * 256, 256), 256)
            block = blocks[part * 256 : (part + 1) * 256, :]
            acc_own += jnp.dot(own_ref[:, tokens], block, preferred_element_type=f32)
            acc_oth += jnp.dot(oth_ref[:, tokens], block, preferred_element_type=f32)
    velocity = beta_decay * mom_ref[...].astype(f32) + acc_own
    v32_ref[0] = velocity
    v16_ref[0] = velocity.astype(bf16)
    goth_ref[...] = acc_oth.astype(bf16)


def grads(scalars, own, oth, blocks, momentum, first, tiles):
    rows, tokens = own.shape
    cols = tiles * TILE
    whole = pl.BlockSpec((rows, tokens), lambda j, s: (0, 0))
    block = pl.BlockSpec((512, TILE), lambda j, s: (0, j))
    mom = pl.BlockSpec((rows, TILE), lambda j, s: (0, s[0] * HALF_TILES + first + j))
    half = pl.BlockSpec((1, rows, TILE), lambda j, s: (0, 0, j))
    return pl.pallas_call(
        grad_kernel,
        grid_spec=pltpu.PrefetchScalarGridSpec(
            num_scalar_prefetch=1,
            grid=(tiles,),
            in_specs=[whole, whole, block, block, block, block, mom],
            out_specs=[half, half, pl.BlockSpec((rows, TILE), lambda j, s: (0, j))],
        ),
        out_shape=[
            jax.ShapeDtypeStruct((2, rows, cols), f32),
            jax.ShapeDtypeStruct((2, rows, cols), bf16),
            jax.ShapeDtypeStruct((rows, cols), bf16),
        ],
        cost_estimate=pl.CostEstimate(
            flops=4 * rows * tokens * cols, bytes_accessed=2 * tokens * cols + 4 * rows * tokens + 10 * rows * cols, transcendentals=0
        ),
        name="grads",
    )(scalars, own, oth, *blocks, momentum)


def other_kernel(s_ref, v32_in, v16_in, grad_ref, mom_ref, v32_ref, v16_ref):
    velocity = beta_decay * mom_ref[...].astype(f32) + grad_ref[...].astype(f32)
    v32_ref[0] = velocity
    v16_ref[0] = velocity.astype(bf16)


def other_half(scalars, v32, v16, grad, momentum, first, tiles):
    rows = grad.shape[0]
    anywhere = pl.BlockSpec(memory_space=pl.ANY)
    half = pl.BlockSpec((1, rows, TILE), lambda j, s: (1, 0, j))
    return pl.pallas_call(
        other_kernel,
        grid_spec=pltpu.PrefetchScalarGridSpec(
            num_scalar_prefetch=1,
            grid=(tiles,),
            in_specs=[
                anywhere,
                anywhere,
                pl.BlockSpec((rows, TILE), lambda j, s: (0, j)),
                pl.BlockSpec((rows, TILE), lambda j, s: (0, (1 - s[0]) * HALF_TILES + first + j)),
            ],
            out_specs=[half, half],
        ),
        out_shape=[jax.ShapeDtypeStruct(v32.shape, f32), jax.ShapeDtypeStruct(v16.shape, bf16)],
        input_output_aliases={1: 0, 2: 1},
        cost_estimate=pl.CostEstimate(flops=2 * grad.size, bytes_accessed=10 * grad.size, transcendentals=0),
        name="other_half",
    )(scalars, v32, v16, grad, momentum)


def final_kernel(s_ref, *refs):
    v1, vb, va, p1, pb, pa, out_p, out_m = refs[-8:]
    velocity = (v1[0] + vb[0].astype(f32) + va[0].astype(f32)) / 3.0
    params = (p1[...] + pb[...].astype(f32) + pa[...].astype(f32)) / 3.0
    out_p[...] = params - learn_rate * velocity
    out_m[...] = velocity.astype(bf16)


def finals(scalars, before, v1, vb, va, p1, pb, pa, first, tiles):
    rows, width = p1.shape
    rel = pl.BlockSpec((1, rows, TILE), lambda half, j, s: (half, 0, j))
    placed = pl.BlockSpec((rows, TILE), lambda half, j, s: (0, (s[0] + half - 2 * s[0] * half) * HALF_TILES + first + j))
    return pl.pallas_call(
        final_kernel,
        grid_spec=pltpu.PrefetchScalarGridSpec(
            num_scalar_prefetch=1,
            grid=(2, tiles),
            in_specs=[pl.BlockSpec(memory_space=pl.ANY)] * len(before) + [rel, rel, rel, placed, placed, placed],
            out_specs=[placed, placed],
        ),
        out_shape=[jax.ShapeDtypeStruct((rows, width), f32), jax.ShapeDtypeStruct((rows, width), bf16)],
        input_output_aliases={1: 0, 2: 1} if before else {},
        cost_estimate=pl.CostEstimate(flops=10 * v1.size, bytes_accessed=22 * v1.size, transcendentals=0),
        name="finals",
    )(scalars, *before, v1, vb, va, p1, pb, pa)


def body(context, out_grad, params, momentum):
    r, t = lax.axis_index("replica"), lax.axis_index("tensor")
    h, y = t // 4, t % 4
    way = 1 - 2 * (r % 2)
    order = [h]
    for step in range(4):
        spot = (y - way * step) % 4
        order += [h * 4 + spot, (1 - h) * 4 + spot]
    scalars = jnp.stack(order).astype(jnp.int32)

    own_ctx = context[0].T
    cot = out_grad[0]
    mom = momentum[0]
    param = params[0]
    width = cot.shape[1]
    half_width = width // 2

    p_sent = param.astype(bf16)
    p_low, p_up = passed_along(p_sent, "replica", 1), passed_along(p_sent, "replica", -1)
    p1 = (param + p_low.astype(f32) + p_up.astype(f32)) / 3.0
    p1_sent = p1.astype(bf16)
    p2_low, p2_up = passed_along(p1_sent, "replica", 2), passed_along(p1_sent, "replica", -2)

    oth_ctx = swap_half(own_ctx)
    done = ()
    for first, tiles in CHUNKS:
        lo, hi = first * TILE, (first + tiles) * TILE
        left, right = cot[:, lo:hi], cot[:, half_width + lo : half_width + hi]
        keep = jnp.where(h == 0, left, right)
        give = jnp.where(h == 0, right, left)
        block = jnp.concatenate([keep, swap_half(give)], 0)
        blocks = [block]
        for _ in range(3):
            blocks.append(ring_step(blocks[-1]))
        v32, v16, g_oth = grads(scalars, own_ctx, oth_ctx, blocks, mom, first, tiles)
        v32, v16 = other_half(scalars, v32, v16, swap_half(g_oth), mom, first, tiles)
        low, up = passed_along(v16, "replica", 1), passed_along(v16, "replica", -1)
        v1 = (v32 + low.astype(f32) + up.astype(f32)) / 3.0
        v1_sent = v1.astype(bf16)
        low2, up2 = passed_along(v1_sent, "replica", 2), passed_along(v1_sent, "replica", -2)
        done = finals(scalars, done, v1, low2, up2, p1, p2_low, p2_up, first, tiles)
    return (done[0][None], done[1][None])


def solution(mesh):
    return jax.shard_map(
        body,
        mesh=mesh,
        in_specs=(
            P("replica", None, "tensor"),
            P("replica", "tensor", None),
            P("replica", "tensor", None),
            P("replica", "tensor", None),
        ),
        out_specs=(P("replica", "tensor", None), P("replica", "tensor", None)),
        check_vma=False,
    )
```

time: 321 us -> 274 us (0.85)
  waiting for transfers between devices: 279 us -> 130 us
  starting transfers between devices: 12.2 us -> 87.3 us
  Pallas kernels: 0 us -> 35.4 us
  between operations: 14.1 us -> 0.76 us
  matrix products: 10.3 us -> 0 us
  other arithmetic: 5.22 us -> 13.5 us
  local copies, waits for them, and re-layouts: 0.01 us -> 4.19 us
    all_gather x1 -> x0, waiting for transfers between devices: 175 us -> none  [body(): gathered = lax.all_gather(out_grad, 'tensor', axis=1, tiled=True)]
    ppermute x0 -> x11, waiting for transfers between devices: none -> 76.4 us  [the longest x5 43.7 us: swap_half(): return lax.ppermute(value, 'tensor', [(t, t ^ 4) for t in range(8)])]
    ppermute x8 -> x12, waiting for transfers between devices: 103 us -> 53.2 us  [passed_along(): return lax.ppermute(value, axis, pairs)]
    ppermute x8 -> x12, starting transfers between devices: 12.2 us -> 59.2 us  [passed_along(): return lax.ppermute(value, axis, pairs)]
    pallas_call x0 -> x6, Pallas kernels: none -> 35.4 us  [the longest x2 14.2 us: finals(): pl.pallas_call(final_kernel, grid_spec=pltpu.PrefetchScalarGridSpec(num_s...]
    ppermute x0 -> x11, starting transfers between devices: none -> 28.1 us  [the longest x5 14.2 us: swap_half(): return lax.ppermute(value, 'tensor', [(t, t ^ 4) for t in range(8)])]
    dot_general x1 -> x0, matrix products: 10.3 us -> none  [body(): lax.dot_general(local_ctx, gathered[0], (((0,), (0,)), ((), ())), preferr...]
    convert_element_type x1 -> x4, other arithmetic: 1.44 us -> 11 us  [the longest x2 4.87 us: body(): v1_sent = v1.astype(bf16)]
  transfers between devices with their start and end apart: 9 -> 23, of which waited for: 7 -> 9; matrix products, arithmetic and copies ran while one was open for 0% -> 5% of each run, Pallas kernels for 0% -> 11%
where the time goes in v1:
time: 274 us; the launch traced here: 271 us
  waiting for transfers between devices  130 us (47%)
  starting transfers between devices  87.3 us (32%)
  Pallas kernels  35.4 us (13%)
  other arithmetic  13.5 us (5%)
  local copies, waits for them, and re-layouts  4.19 us (2%)
    ppermute x12, starting transfers between devices, passed_along(): return lax.ppermute(value, axis, pairs)  59.2 us
    ppermute x12, waiting for transfers between devices, passed_along(): return lax.ppermute(value, axis, pairs)  53.2 us
    ppermute x5, waiting for transfers between devices, swap_half(): return lax.ppermute(value, 'tensor', [(t, t ^ 4) for t in range(8)])  43.7 us
    ppermute x6, waiting for transfers between devices, ring_step(): return lax.ppermute(value, BOTH, pairs)  32.7 us
    pallas_call x2, Pallas kernels, finals(): pl.pallas_call(final_kernel, grid_spec=pltpu.PrefetchScalarGridSpec(num_s...  14.2 us
    ppermute x5, starting transfers between devices, swap_half(): return lax.ppermute(value, 'tensor', [(t, t ^ 4) for t in range(8)])  14.2 us
    ppermute x6, starting transfers between devices, ring_step(): return lax.ppermute(value, BOTH, pairs)  13.9 us
    pallas_call x2, Pallas kernels, grads(): pl.pallas_call(grad_kernel, grid_spec=pltpu.PrefetchScalarGridSpec(num_sc...  13.2 us
  transfers between devices with their start and end apart: 23, of which 9 were waited for; matrix products, arithmetic and copies ran while one was open for 5% of the time, Pallas kernels for 11%

profile of v1, /device:TPU:1, one launch (start us, length us, event | category | flops | bytes accessed | tf_op | source)
XLA Modules:
  0.0 270.9 jit_solution(10095240011408444901)
XLA Ops:
  0.6 1.3 broadcast_select_fusion.1
  1.9 3.7 %collective-permute-start.1 = (bf16[256,1024]{1,0:T(8,128)(2,1)S(1)}, bf16[256,1024]{1,0:T(8,128)(2,1)S(1)}, u32[]{:S(2)}, u32[]{:S(2)}) collective-permute-start(bf16[256,1024]{1,0:T(8,128)(2,1)S(1)} %get-tuple-element.39), channel_id=1, source_target_pairs={{0,4},{1,5},{2,6},{3,7},{4,0},{5,1},{6,2},{7,3},{8,12},{9,13},{10,... | collective-permute-start | bytes 1572872 | tf_op jit(solution)/shard_map/ppermute | solution.py:27
  5.6 10.6 %collective-permute-done.1 = bf16[256,1024]{1,0:T(8,128)(2,1)S(1)} collective-permute-done((bf16[256,1024]{1,0:T(8,128)(2,1)S(1)}, bf16[256,1024]{1,0:T(8,128)(2,1)S(1)}, u32[]{:S(2)}, u32[]{:S(2)}) %collective-permute-start.1) | collective-permute-done | bytes 524320 | tf_op jit(solution)/shard_map/ppermute | solution.py:27
  16.2 0.1 pad_maximum_fusion.g0
  16.3 1.0 copy-done.4
  17.2 3.7 %collective-permute-start.2 = (bf16[512,1024]{1,0:T(8,128)(2,1)S(1)}, bf16[512,1024]{1,0:T(8,128)(2,1)S(1)}, u32[]{:S(2)}, u32[]{:S(2)}) collective-permute-start(bf16[512,1024]{1,0:T(8,128)(2,1)S(1)} %pad_maximum_fusion.g0), channel_id=1, source_target_pairs={{0,1},{1,2},{2,3},{3,0},{4,5},{5,6},{6,7},{7,4},{8,11},{9,8},{10,9... | collective-permute-start | bytes 3145736 | tf_op jit(solution)/shard_map/ppermute | solution.py:36
  20.9 11.7 %collective-permute-done.2.g1 = bf16[512,1024]{1,0:T(8,128)(2,1)S(1)} collective-permute-done((bf16[512,1024]{1,0:T(8,128)(2,1)S(1)}, bf16[512,1024]{1,0:T(8,128)(2,1)S(1)}, u32[]{:S(2)}, u32[]{:S(2)}) %collective-permute-start.2) | collective-permute-done | bytes 1048608 | tf_op jit(solution)/shard_map/ppermute | solution.py:36
  32.7 3.1 %collective-permute-start.3 = (bf16[512,1024]{1,0:T(8,128)(2,1)S(1)}, bf16[512,1024]{1,0:T(8,128)(2,1)}, u32[]{:S(2)}, u32[]{:S(2)}) collective-permute-start(bf16[512,1024]{1,0:T(8,128)(2,1)S(1)} %collective-permute-done.2.g1), channel_id=1, source_target_pairs={{0,1},{1,2},{2,3},{3,0},{4,5},{5,6},{6,7},{7,4},{8,11},{9,8},{10,9... | collective-permute-start | bytes 3145736 | tf_op jit(solution)/shard_map/ppermute | solution.py:36
  35.8 1.2 broadcast_select_fusion.3
  37.0 2.8 %collective-permute-start.14 = (bf16[256,768]{1,0:T(8,128)(2,1)S(1)}, bf16[256,768]{1,0:T(8,128)(2,1)S(1)}, u32[]{:S(2)}, u32[]{:S(2)}) collective-permute-start(bf16[256,768]{1,0:T(8,128)(2,1)S(1)} %get-tuple-element.37), channel_id=1, source_target_pairs={{0,4},{1,5},{2,6},{3,7},{4,0},{5,1},{6,2},{7,3},{8,12},{9,13},{10,... | collective-permute-start | bytes 1179656 | tf_op jit(solution)/shard_map/ppermute | solution.py:27
  39.8 1.3 bitcast_convert_fusion
  41.1 0.6 collective-permute-start.11
  41.7 1.5 collective-permute-start.10
  43.2 4.3 %collective-permute-done.3.g2 = bf16[512,1024]{1,0:T(8,128)(2,1)} collective-permute-done((bf16[512,1024]{1,0:T(8,128)(2,1)S(1)}, bf16[512,1024]{1,0:T(8,128)(2,1)}, u32[]{:S(2)}, u32[]{:S(2)}) %collective-permute-start.3) | collective-permute-done | bytes 1048608 | tf_op jit(solution)/shard_map/ppermute | solution.py:36
  47.5 3.2 %collective-permute-start.4 = (bf16[512,1024]{1,0:T(8,128)(2,1)}, bf16[512,1024]{1,0:T(8,128)(2,1)}, u32[]{:S(2)}, u32[]{:S(2)}) collective-permute-start(bf16[512,1024]{1,0:T(8,128)(2,1)} %collective-permute-done.3.g2), channel_id=1, source_target_pairs={{0,1},{1,2},{2,3},{3,0},{4,5},{5,6},{6,7},{7,4},{8,11},{9,8},{10,9... | collective-permute-start | bytes 3145736 | tf_op jit(solution)/shard_map/ppermute | solution.py:36
  50.8 0.1 pad_maximum_fusion.1.g0
  50.8 0.9 copy-done.5
  51.7 0.0 collective-permute-start.15
  51.7 2.7 %collective-permute-start = (bf16[224,2048]{1,0:T(8,128)(2,1)}, bf16[224,2048]{1,0:T(8,128)(2,1)}, u32[]{:S(2)}, u32[]{:S(2)}) collective-permute-start(bf16[224,2048]{1,0:T(8,128)(2,1)} %bitcast.10.own_ref), channel_id=1, source_target_pairs={{0,4},{1,5},{2,6},{3,7},{4,0},{5,1},{6,2},{7,3},{8,12},{9,13},{10,... | collective-permute-start | bytes 2752520 | tf_op jit(solution)/shard_map/ppermute | solution.py:27
  54.5 16.7 %collective-permute-done.15.g1 = bf16[512,768]{1,0:T(8,128)(2,1)} collective-permute-done((bf16[512,768]{1,0:T(8,128)(2,1)S(1)}, bf16[512,768]{1,0:T(8,128)(2,1)}, u32[]{:S(2)}, u32[]{:S(2)}) %collective-permute-start.15) | collective-permute-done | bytes 786464 | tf_op jit(solution)/shard_map/ppermute | solution.py:36
  71.1 3.5 %collective-permute-start.16 = (bf16[512,768]{1,0:T(8,128)(2,1)}, bf16[512,768]{1,0:T(8,128)(2,1)}, u32[]{:S(2)}, u32[]{:S(2)}) collective-permute-start(bf16[512,768]{1,0:T(8,128)(2,1)} %collective-permute-done.15.g1), channel_id=1, source_target_pairs={{0,1},{1,2},{2,3},{3,0},{4,5},{5,6},{6,7},{7,4},{8,11},{9,8},{10,9... | collective-permute-start | bytes 2359304 | tf_op jit(solution)/shard_map/ppermute | solution.py:36
  74.7 0.6 stack.39.s_ref
  75.3 13.5 %collective-permute-done.oth_ref = bf16[224,2048]{1,0:T(8,128)(2,1)} collective-permute-done((bf16[224,2048]{1,0:T(8,128)(2,1)}, bf16[224,2048]{1,0:T(8,128)(2,1)}, u32[]{:S(2)}, u32[]{:S(2)}) %collective-permute-start) | collective-permute-done | bytes 917536 | tf_op jit(solution)/shard_map/ppermute | solution.py:27
  88.8 7.0 %grads.2 = (f32[2,224,1024]{2,1,0:T(8,128)}, bf16[2,224,1024]{2,1,0:T(8,128)(2,1)}, bf16[224,1024]{1,0:T(8,128)(2,1)}) custom-call(s32[9]{0:T(128)} %stack.39.s_ref, bf16[224,2048]{1,0:T(8,128)(2,1)} %bitcast.10.own_ref, bf16[224,2048]{1,0:T(8,128)(2,1)} %collective-permute-done.oth_ref, bf16[512,1024]{1,0:T(8,128)(2,1)} %copy-done.4, ...), custom_call_target="tpu_custom_call" | custom-call | flops 1879048192 | bytes 8323072 | tf_op jit(solution)/shard_map/grads/pallas_call | solution.py:61
  95.8 2.8 %collective-permute-start.5 = (bf16[224,1024]{1,0:T(8,128)(2,1)}, bf16[224,1024]{1,0:T(8,128)(2,1)}, u32[]{:S(2)}, u32[]{:S(2)}) collective-permute-start(bf16[224,1024]{1,0:T(8,128)(2,1)} %get-tuple-element.18), channel_id=1, source_target_pairs={{0,4},{1,5},{2,6},{3,7},{4,0},{5,1},{6,2},{7,3},{8,12},{9,13},{10,... | collective-permute-start | bytes 1376264 | tf_op jit(solution)/shard_map/ppermute | solution.py:27
  98.6 0.4 collective-permute-start.17
  99.0 10.3 %collective-permute-done.5.grad_ref = bf16[224,1024]{1,0:T(8,128)(2,1)} collective-permute-done((bf16[224,1024]{1,0:T(8,128)(2,1)}, bf16[224,1024]{1,0:T(8,128)(2,1)}, u32[]{:S(2)}, u32[]{:S(2)}) %collective-permute-start.5) | collective-permute-done | bytes 458784 | tf_op jit(solution)/shard_map/ppermute | solution.py:27
  109.2 4.2 %other_half.2 = (f32[2,224,1024]{2,1,0:T(8,128)}, bf16[2,224,1024]{2,1,0:T(8,128)(2,1)}) custom-call(s32[9]{0:T(128)} %stack.39.s_ref, f32[2,224,1024]{2,1,0:T(8,128)} %get-tuple-element.16.v32_in, bf16[2,224,1024]{2,1,0:T(8,128)(2,1)} %get-tuple-element.17.v16_in, ...), custom_call_target="tpu_custom_call", output_to_operand_aliasing={{0}: (1, {}), {1}: (2, {})} | custom-call | flops 458752 | bytes 2293760 | tf_op jit(solution)/shard_map/other_half/pallas_call | solution.py:91
  113.4 1.4 collective-permute-start.7
  114.7 0.4 collective-permute-start.6
  115.1 4.8 %fusion.3 = (bf16[224,3584]{1,0:T(8,128)(2,1)}, f32[224,3584]{1,0:T(8,128)}) fusion(bf16[224,3584]{1,0:T(8,128)(2,1)} %collective-permute-done.11, bf16[224,3584]{1,0:T(8,128)(2,1)} %collective-permute-done.10, f32[1,224,3584]{2,1,0:T(8,128)S(1)} %copy-done), kind=kLoop, calls=%fused_computation.13 | loop fusion | flops 4816896 | bytes 11239424 | tf_op jit(solution)/shard_map/convert_element_type | solution.py:158
  119.9 8.1 %collective-permute-start.13 = (bf16[224,3584]{1,0:T(8,128)(2,1)}, bf16[224,3584]{1,0:T(8,128)(2,1)S(1)}, u32[]{:S(2)}, u32[]{:S(2)}) collective-permute-start(bf16[224,3584]{1,0:T(8,128)(2,1)} %get-tuple-element.32), channel_id=1, source_target_pairs={{0,240},{8,248},{16,0},{24,8},{32,16},{40,24},{48,32},{56,40},{64,... | collective-permute-start | bytes 4816904 | tf_op jit(solution)/shard_map/ppermute | solution.py:23
  128.0 6.2 %grads.3 = (f32[2,224,768]{2,1,0:T(8,128)}, bf16[2,224,768]{2,1,0:T(8,128)(2,1)}, bf16[224,768]{1,0:T(8,128)(2,1)}) custom-call(s32[9]{0:T(128)} %stack.39.s_ref, bf16[224,2048]{1,0:T(8,128)(2,1)} %bitcast.10.own_ref, bf16[224,2048]{1,0:T(8,128)(2,1)} %collective-permute-done.oth_ref, bf16[512,768]{1,0:T(8,128)(2,1)} %copy-done.5, ...), custom_call_target="tpu_custom_call" | custom-call | flops 1409286144 | bytes 6701056 | tf_op jit(solution)/shard_map/grads/pallas_call | solution.py:61
  134.2 2.1 collective-permute-start.18
  136.4 9.3 %collective-permute-done.18.grad_ref = bf16[224,768]{1,0:T(8,128)(2,1)S(1)} collective-permute-done((bf16[224,768]{1,0:T(8,128)(2,1)}, bf16[224,768]{1,0:T(8,128)(2,1)S(1)}, u32[]{:S(2)}, u32[]{:S(2)}) %collective-permute-start.18) | collective-permute-done | bytes 344096 | tf_op jit(solution)/shard_map/ppermute | solution.py:27
  145.7 0.7 copy-done.9
  146.5 3.8 %other_half.3 = (f32[2,224,768]{2,1,0:T(8,128)}, bf16[2,224,768]{2,1,0:T(8,128)(2,1)}) custom-call(s32[9]{0:T(128)} %stack.39.s_ref, f32[2,224,768]{2,1,0:T(8,128)} %get-tuple-element.23.v32_in, bf16[2,224,768]{2,1,0:T(8,128)(2,1)} %get-tuple-element.24.v16_in, bf16[224,768]{1,0:T(8,128)(2,1)} %copy-done.9, ...), custom_call_target="tpu_custom_call", output_to_operand_aliasing={{0}: (1, {}), {1}: (2, {})} | custom-call | flops 344064 | bytes 1720320 | tf_op jit(solution)/shard_map/other_half/pallas_call | solution.py:91
  150.3 0.7 collective-permute-start.20
  151.0 1.0 collective-permute-start.19
  152.1 3.3 %fusion.5 = (bf16[2,224,1024]{2,1,0:T(8,128)(2,1)S(1)}, f32[2,224,1024]{2,1,0:T(8,128)}) fusion(bf16[2,224,1024]{2,1,0:T(8,128)(2,1)} %collective-permute-done.7, f32[2,224,1024]{2,1,0:T(8,128)S(1)} %copy-done.1, bf16[2,224,1024]{2,1,0:T(8,128)(2,1)} %collective-permute-done.6), kind=kLoop, calls=%fused_computation.14 | loop fusion | flops 2752512 | bytes 6422528 | tf_op jit(solution)/shard_map/convert_element_type | solution.py:176
  155.3 33.8 %collective-permute-start.9 = (bf16[2,224,1024]{2,1,0:T(8,128)(2,1)S(1)}, bf16[2,224,1024]{2,1,0:T(8,128)(2,1)S(1)}, u32[]{:S(2)}, u32[]{:S(2)}) collective-permute-start(bf16[2,224,1024]{2,1,0:T(8,128)(2,1)S(1)} %get-tuple-element.34), channel_id=1, source_target_pairs={{0,240},{8,248},{16,0},{24,8},{32,16},{40,24},{48,32},{56,40},{64,... | collective-permute-start | bytes 2752520 | tf_op jit(solution)/shard_map/ppermute | solution.py:23
  189.2 1.6 fusion.2
  190.8 11.7 %collective-permute-start.22 = (bf16[2,224,768]{2,1,0:T(8,128)(2,1)}, bf16[2,224,768]{2,1,0:T(8,128)(2,1)}, u32[]{:S(2)}, u32[]{:S(2)}) collective-permute-start(bf16[2,224,768]{2,1,0:T(8,128)(2,1)} %get-tuple-element.30), channel_id=1, source_target_pairs={{0,240},{8,248},{16,0},{24,8},{32,16},{40,24},{48,32},{56,40},{64,... | collective-permute-start | bytes 2064392 | tf_op jit(solution)/shard_map/ppermute | solution.py:23
  202.5 33.4 %collective-permute-done.12.refs_4_.refs_6_ = bf16[224,3584]{1,0:T(8,128)(2,1)} collective-permute-done((bf16[224,3584]{1,0:T(8,128)(2,1)}, bf16[224,3584]{1,0:T(8,128)(2,1)}, u32[]{:S(2)}, u32[]{:S(2)}) %collective-permute-start.12) | collective-permute-done | bytes 1605664 | tf_op jit(solution)/shard_map/ppermute | solution.py:23
  235.9 19.8 %collective-permute-done.8.refs_1_ = bf16[2,224,1024]{2,1,0:T(8,128)(2,1)S(1)} collective-permute-done((bf16[2,224,1024]{2,1,0:T(8,128)(2,1)S(1)}, bf16[2,224,1024]{2,1,0:T(8,128)(2,1)S(1)}, u32[]{:S(2)}, u32[]{:S(2)}) %collective-permute-start.8) | collective-permute-done | bytes 917536 | tf_op jit(solution)/shard_map/ppermute | solution.py:23
  255.7 0.9 copy-done.8
  256.6 7.8 %finals.2 = (f32[224,3584]{1,0:T(8,128)}, bf16[224,3584]{1,0:T(8,128)(2,1)}) custom-call(s32[9]{0:T(128)} %stack.39.s_ref, f32[2,224,1024]{2,1,0:T(8,128)} %get-tuple-element.35.refs_0_, bf16[2,224,1024]{2,1,0:T(8,128)(2,1)} %copy-done.8, bf16[2,224,1024]{2,1,0:T(8,128)(2,1)} %copy-done.7, f32[224,3584]{1,0:T(8,128)} %get-tuple-element.33.refs_3_.refs_5_, ...), custom_call_target="tpu_custom_call" | custom-call | flops 4587520 | bytes 10092544 | tf_op jit(solution)/shard_map/finals/pallas_call | solution.py:123
  264.5 6.4 %finals.3 = (f32[224,3584]{1,0:T(8,128)}, bf16[224,3584]{1,0:T(8,128)(2,1)}) custom-call(s32[9]{0:T(128)} %stack.39.s_ref, f32[224,3584]{1,0:T(8,128)} %get-tuple-element.21.refs_0_, bf16[224,3584]{1,0:T(8,128)(2,1)} %get-tuple-element.22.refs_1_, f32[2,224,768]{2,1,0:T(8,128)} %get-tuple-element.31.refs_2_, ...), custom_call_target="tpu_custom_call", output_to_operand_aliasing={{0}: (1, {}), {1}: (2, {})} | custom-call | flops 3440640 | bytes 7569408 | tf_op jit(solution)/shard_map/finals/pallas_call | solution.py:123
  (33 shorter events, 0.1 us)
Async XLA Ops:
  1.9 14.3 %collective-permute-start.1 = (bf16[256,1024]{1,0:T(8,128)(2,1)S(1)}, bf16[256,1024]{1,0:T(8,128)(2,1)S(1)}, u32[]{:S(2)}, u32[]{:S(2)}) collective-permute-start(bf16[256,1024]{1,0:T(8,128)(2,1)S(1)} %get-tuple-element.39), channel_id=1, source_target_pairs={{0,4},{1,5},{2,6},{3,7},{4,0},{5,1},{6,2},{7,3},{8,12},{9,13},{10,... | collective-permute-start | bytes 1572872 | tf_op jit(solution)/shard_map/ppermute | solution.py:27
  16.2 23.6 %copy-start = (f32[1,224,3584]{2,1,0:T(8,128)S(1)}, f32[1,224,3584]{2,1,0:T(8,128)}, u32[]{:S(2)}) copy-start(f32[1,224,3584]{2,1,0:T(8,128)} %param.6) | copy-start | bytes 9633796
  16.3 1.0 copy-start.4
  17.2 15.4 %collective-permute-start.2 = (bf16[512,1024]{1,0:T(8,128)(2,1)S(1)}, bf16[512,1024]{1,0:T(8,128)(2,1)S(1)}, u32[]{:S(2)}, u32[]{:S(2)}) collective-permute-start(bf16[512,1024]{1,0:T(8,128)(2,1)S(1)} %pad_maximum_fusion.g0), channel_id=1, source_target_pairs={{0,1},{1,2},{2,3},{3,0},{4,5},{5,6},{6,7},{7,4},{8,11},{9,8},{10,9... | collective-permute-start | bytes 3145736 | tf_op jit(solution)/shard_map/ppermute | solution.py:36
  32.7 8.4 %copy-start.6 = (bf16[512,1024]{1,0:T(8,128)(2,1)}, bf16[512,1024]{1,0:T(8,128)(2,1)S(1)}, u32[]{:S(2)}) copy-start(bf16[512,1024]{1,0:T(8,128)(2,1)S(1)} %collective-permute-done.2.g1) | copy-start | bytes 3145732
  32.7 14.9 %collective-permute-start.3 = (bf16[512,1024]{1,0:T(8,128)(2,1)S(1)}, bf16[512,1024]{1,0:T(8,128)(2,1)}, u32[]{:S(2)}, u32[]{:S(2)}) collective-permute-start(bf16[512,1024]{1,0:T(8,128)(2,1)S(1)} %collective-permute-done.2.g1), channel_id=1, source_target_pairs={{0,1},{1,2},{2,3},{3,0},{4,5},{5,6},{6,7},{7,4},{8,11},{9,8},{10,9... | collective-permute-start | bytes 3145736 | tf_op jit(solution)/shard_map/ppermute | solution.py:36
  37.0 13.8 %collective-permute-start.14 = (bf16[256,768]{1,0:T(8,128)(2,1)S(1)}, bf16[256,768]{1,0:T(8,128)(2,1)S(1)}, u32[]{:S(2)}, u32[]{:S(2)}) collective-permute-start(bf16[256,768]{1,0:T(8,128)(2,1)S(1)} %get-tuple-element.37), channel_id=1, source_target_pairs={{0,4},{1,5},{2,6},{3,7},{4,0},{5,1},{6,2},{7,3},{8,12},{9,13},{10,... | collective-permute-start | bytes 1179656 | tf_op jit(solution)/shard_map/ppermute | solution.py:27
  41.1 74.0 %collective-permute-start.11 = (bf16[224,3584]{1,0:T(8,128)(2,1)}, bf16[224,3584]{1,0:T(8,128)(2,1)}, u32[]{:S(2)}, u32[]{:S(2)}) collective-permute-start(bf16[224,3584]{1,0:T(8,128)(2,1)} %bitcast_convert_fusion), channel_id=1, source_target_pairs={{0,248},{8,0},{16,8},{24,16},{32,24},{40,32},{48,40},{56,48},{64,5... | collective-permute-start | bytes 4816904 | tf_op jit(solution)/shard_map/ppermute | solution.py:23
  41.7 73.4 %collective-permute-start.10 = (bf16[224,3584]{1,0:T(8,128)(2,1)}, bf16[224,3584]{1,0:T(8,128)(2,1)}, u32[]{:S(2)}, u32[]{:S(2)}) collective-permute-start(bf16[224,3584]{1,0:T(8,128)(2,1)} %bitcast_convert_fusion), channel_id=1, source_target_pairs={{0,8},{8,16},{16,24},{24,32},{32,40},{40,48},{48,56},{56,64},{64,7... | collective-permute-start | bytes 4816904 | tf_op jit(solution)/shard_map/ppermute | solution.py:23
  47.5 41.3 %collective-permute-start.4 = (bf16[512,1024]{1,0:T(8,128)(2,1)}, bf16[512,1024]{1,0:T(8,128)(2,1)}, u32[]{:S(2)}, u32[]{:S(2)}) collective-permute-start(bf16[512,1024]{1,0:T(8,128)(2,1)} %collective-permute-done.3.g2), channel_id=1, source_target_pairs={{0,1},{1,2},{2,3},{3,0},{4,5},{5,6},{6,7},{7,4},{8,11},{9,8},{10,9... | collective-permute-start | bytes 3145736 | tf_op jit(solution)/shard_map/ppermute | solution.py:36
  50.8 0.9 copy-start.5
  51.7 19.4 %collective-permute-start.15 = (bf16[512,768]{1,0:T(8,128)(2,1)S(1)}, bf16[512,768]{1,0:T(8,128)(2,1)}, u32[]{:S(2)}, u32[]{:S(2)}) collective-permute-start(bf16[512,768]{1,0:T(8,128)(2,1)S(1)} %pad_maximum_fusion.1.g0), channel_id=1, source_target_pairs={{0,1},{1,2},{2,3},{3,0},{4,5},{5,6},{6,7},{7,4},{8,11},{9,8},{10,9... | collective-permute-start | bytes 2359304 | tf_op jit(solution)/shard_map/ppermute | solution.py:36
  51.7 37.1 %collective-permute-start = (bf16[224,2048]{1,0:T(8,128)(2,1)}, bf16[224,2048]{1,0:T(8,128)(2,1)}, u32[]{:S(2)}, u32[]{:S(2)}) collective-permute-start(bf16[224,2048]{1,0:T(8,128)(2,1)} %bitcast.10.own_ref), channel_id=1, source_target_pairs={{0,4},{1,5},{2,6},{3,7},{4,0},{5,1},{6,2},{7,3},{8,12},{9,13},{10,... | collective-permute-start | bytes 2752520 | tf_op jit(solution)/shard_map/ppermute | solution.py:27
  71.1 27.4 %collective-permute-start.16 = (bf16[512,768]{1,0:T(8,128)(2,1)}, bf16[512,768]{1,0:T(8,128)(2,1)}, u32[]{:S(2)}, u32[]{:S(2)}) collective-permute-start(bf16[512,768]{1,0:T(8,128)(2,1)} %collective-permute-done.15.g1), channel_id=1, source_target_pairs={{0,1},{1,2},{2,3},{3,0},{4,5},{5,6},{6,7},{7,4},{8,11},{9,8},{10,9... | collective-permute-start | bytes 2359304 | tf_op jit(solution)/shard_map/ppermute | solution.py:36
  95.8 13.4 %collective-permute-start.5 = (bf16[224,1024]{1,0:T(8,128)(2,1)}, bf16[224,1024]{1,0:T(8,128)(2,1)}, u32[]{:S(2)}, u32[]{:S(2)}) collective-permute-start(bf16[224,1024]{1,0:T(8,128)(2,1)} %get-tuple-element.18), channel_id=1, source_target_pairs={{0,4},{1,5},{2,6},{3,7},{4,0},{5,1},{6,2},{7,3},{8,12},{9,13},{10,... | collective-permute-start | bytes 1376264 | tf_op jit(solution)/shard_map/ppermute | solution.py:27
  98.6 29.4 %collective-permute-start.17 = (bf16[512,768]{1,0:T(8,128)(2,1)}, bf16[512,768]{1,0:T(8,128)(2,1)}, u32[]{:S(2)}, u32[]{:S(2)}) collective-permute-start(bf16[512,768]{1,0:T(8,128)(2,1)} %collective-permute-done.16.g2), channel_id=1, source_target_pairs={{0,1},{1,2},{2,3},{3,0},{4,5},{5,6},{6,7},{7,4},{8,11},{9,8},{10,9... | collective-permute-start | bytes 2359304 | tf_op jit(solution)/shard_map/ppermute | solution.py:36
  113.4 38.6 %collective-permute-start.7 = (bf16[2,224,1024]{2,1,0:T(8,128)(2,1)}, bf16[2,224,1024]{2,1,0:T(8,128)(2,1)}, u32[]{:S(2)}, u32[]{:S(2)}) collective-permute-start(bf16[2,224,1024]{2,1,0:T(8,128)(2,1)} %get-tuple-element.20), channel_id=1, source_target_pairs={{0,248},{8,0},{16,8},{24,16},{32,24},{40,32},{48,40},{56,48},{64,5... | collective-permute-start | bytes 2752520 | tf_op jit(solution)/shard_map/ppermute | solution.py:23
  114.7 37.3 %collective-permute-start.6 = (bf16[2,224,1024]{2,1,0:T(8,128)(2,1)}, bf16[2,224,1024]{2,1,0:T(8,128)(2,1)}, u32[]{:S(2)}, u32[]{:S(2)}) collective-permute-start(bf16[2,224,1024]{2,1,0:T(8,128)(2,1)} %get-tuple-element.20), channel_id=1, source_target_pairs={{0,8},{8,16},{16,24},{24,32},{32,40},{40,48},{48,56},{56,64},{64,7... | collective-permute-start | bytes 2752520 | tf_op jit(solution)/shard_map/ppermute | solution.py:23
  119.9 82.6 %collective-permute-start.13 = (bf16[224,3584]{1,0:T(8,128)(2,1)}, bf16[224,3584]{1,0:T(8,128)(2,1)S(1)}, u32[]{:S(2)}, u32[]{:S(2)}) collective-permute-start(bf16[224,3584]{1,0:T(8,128)(2,1)} %get-tuple-element.32), channel_id=1, source_target_pairs={{0,240},{8,248},{16,0},{24,8},{32,16},{40,24},{48,32},{56,40},{64,... | collective-permute-start | bytes 4816904 | tf_op jit(solution)/shard_map/ppermute | solution.py:23
  134.2 11.5 %collective-permute-start.18 = (bf16[224,768]{1,0:T(8,128)(2,1)}, bf16[224,768]{1,0:T(8,128)(2,1)S(1)}, u32[]{:S(2)}, u32[]{:S(2)}) collective-permute-start(bf16[224,768]{1,0:T(8,128)(2,1)} %get-tuple-element.25), channel_id=1, source_target_pairs={{0,4},{1,5},{2,6},{3,7},{4,0},{5,1},{6,2},{7,3},{8,12},{9,13},{10,... | collective-permute-start | bytes 1032200 | tf_op jit(solution)/shard_map/ppermute | solution.py:27
  145.7 0.7 copy-start.9
  146.5 5.6 %copy-start.1 = (f32[2,224,1024]{2,1,0:T(8,128)S(1)}, f32[2,224,1024]{2,1,0:T(8,128)}, u32[]{:S(2)}) copy-start(f32[2,224,1024]{2,1,0:T(8,128)} %get-tuple-element.19) | copy-start | bytes 5505028
  150.3 38.9 %collective-permute-start.20 = (bf16[2,224,768]{2,1,0:T(8,128)(2,1)}, bf16[2,224,768]{2,1,0:T(8,128)(2,1)S(1)}, u32[]{:S(2)}, u32[]{:S(2)}) collective-permute-start(bf16[2,224,768]{2,1,0:T(8,128)(2,1)} %get-tuple-element.27), channel_id=1, source_target_pairs={{0,248},{8,0},{16,8},{24,16},{32,24},{40,32},{48,40},{56,48},{64,5... | collective-permute-start | bytes 2064392 | tf_op jit(solution)/shard_map/ppermute | solution.py:23
  151.0 38.2 %collective-permute-start.19 = (bf16[2,224,768]{2,1,0:T(8,128)(2,1)}, bf16[2,224,768]{2,1,0:T(8,128)(2,1)S(1)}, u32[]{:S(2)}, u32[]{:S(2)}) collective-permute-start(bf16[2,224,768]{2,1,0:T(8,128)(2,1)} %get-tuple-element.27), channel_id=1, source_target_pairs={{0,8},{8,16},{16,24},{24,32},{32,40},{40,48},{48,56},{56,64},{64,7... | collective-permute-start | bytes 2064392 | tf_op jit(solution)/shard_map/ppermute | solution.py:23
  152.0 83.9 %collective-permute-start.12 = (bf16[224,3584]{1,0:T(8,128)(2,1)}, bf16[224,3584]{1,0:T(8,128)(2,1)}, u32[]{:S(2)}, u32[]{:S(2)}) collective-permute-start(bf16[224,3584]{1,0:T(8,128)(2,1)} %get-tuple-element.32), channel_id=1, source_target_pairs={{0,16},{8,24},{16,32},{24,40},{32,48},{40,56},{48,64},{56,72},{64,... | collective-permute-start | bytes 4816904 | tf_op jit(solution)/shard_map/ppermute | solution.py:23
  152.1 37.1 %copy-start.3 = (f32[2,224,768]{2,1,0:T(8,128)S(1)}, f32[2,224,768]{2,1,0:T(8,128)}, u32[]{:S(2)}) copy-start(f32[2,224,768]{2,1,0:T(8,128)} %get-tuple-element.26) | copy-start | bytes 4128772
  155.3 80.6 %collective-permute-start.9 = (bf16[2,224,1024]{2,1,0:T(8,128)(2,1)S(1)}, bf16[2,224,1024]{2,1,0:T(8,128)(2,1)S(1)}, u32[]{:S(2)}, u32[]{:S(2)}) collective-permute-start(bf16[2,224,1024]{2,1,0:T(8,128)(2,1)S(1)} %get-tuple-element.34), channel_id=1, source_target_pairs={{0,240},{8,248},{16,0},{24,8},{32,16},{40,24},{48,32},{56,40},{64,... | collective-permute-start | bytes 2752520 | tf_op jit(solution)/shard_map/ppermute | solution.py:23
  189.2 66.5 %collective-permute-start.8 = (bf16[2,224,1024]{2,1,0:T(8,128)(2,1)S(1)}, bf16[2,224,1024]{2,1,0:T(8,128)(2,1)S(1)}, u32[]{:S(2)}, u32[]{:S(2)}) collective-permute-start(bf16[2,224,1024]{2,1,0:T(8,128)(2,1)S(1)} %get-tuple-element.34), channel_id=1, source_target_pairs={{0,16},{8,24},{16,32},{24,40},{32,48},{40,56},{48,64},{56,72},{64,... | collective-permute-start | bytes 2752520 | tf_op jit(solution)/shard_map/ppermute | solution.py:23
  190.8 73.7 %collective-permute-start.22 = (bf16[2,224,768]{2,1,0:T(8,128)(2,1)}, bf16[2,224,768]{2,1,0:T(8,128)(2,1)}, u32[]{:S(2)}, u32[]{:S(2)}) collective-permute-start(bf16[2,224,768]{2,1,0:T(8,128)(2,1)} %get-tuple-element.30), channel_id=1, source_target_pairs={{0,240},{8,248},{16,0},{24,8},{32,16},{40,24},{48,32},{56,40},{64,... | collective-permute-start | bytes 2064392 | tf_op jit(solution)/shard_map/ppermute | solution.py:23
  202.5 53.2 %copy-start.2 = (bf16[224,3584]{1,0:T(8,128)(2,1)}, bf16[224,3584]{1,0:T(8,128)(2,1)S(1)}, u32[]{:S(2)}) copy-start(bf16[224,3584]{1,0:T(8,128)(2,1)S(1)} %collective-permute-done.13.refs_5_.refs_7_) | copy-start | bytes 4816900
  202.5 62.0 %collective-permute-start.21 = (bf16[2,224,768]{2,1,0:T(8,128)(2,1)}, bf16[2,224,768]{2,1,0:T(8,128)(2,1)}, u32[]{:S(2)}, u32[]{:S(2)}) collective-permute-start(bf16[2,224,768]{2,1,0:T(8,128)(2,1)} %get-tuple-element.30), channel_id=1, source_target_pairs={{0,16},{8,24},{16,32},{24,40},{32,48},{40,56},{48,64},{56,72},{64,... | collective-permute-start | bytes 2064392 | tf_op jit(solution)/shard_map/ppermute | solution.py:23
  235.9 19.8 %copy-start.7 = (bf16[2,224,1024]{2,1,0:T(8,128)(2,1)}, bf16[2,224,1024]{2,1,0:T(8,128)(2,1)S(1)}, u32[]{:S(2)}) copy-start(bf16[2,224,1024]{2,1,0:T(8,128)(2,1)S(1)} %collective-permute-done.9.refs_2_) | copy-start | bytes 2752516
  255.7 0.9 copy-start.8

commit v2 on v0

v2 whole, which is shorter than its diff:
```python
import jax
import jax.numpy as jnp
from jax import lax
from jax.sharding import PartitionSpec as P

learn_rate = 0.01
beta_decay = 0.9

BOTH = ("replica", "tensor")
CUTS = ((0, 2048), (2048, 3584))
bf16, f32 = jnp.bfloat16, jnp.float32


def passed_along(value, steps):
    pairs = [(source, (source + steps) % 32) for source in range(32)]
    return lax.ppermute(value, "replica", pairs)


def swapped(value):
    return lax.ppermute(value, "tensor", [(t, t ^ 4) for t in range(8)])


def ring_step(value):
    pairs = []
    for r in range(32):
        way = 1 if r % 2 == 0 else -1
        for t in range(8):
            pairs.append((r * 8 + t, r * 8 + (t & 4) + ((t + way) & 3)))
    return lax.ppermute(value, BOTH, pairs)


def tied(*values):
    return lax.optimization_barrier(values)


def third(own, below, above):
    return (own + below.astype(f32) + above.astype(f32)) / 3.0


def body(context, out_grad, params, momentum):
    r, t = lax.axis_index("replica"), lax.axis_index("tensor")
    h, y = t >> 2, t & 3
    way = 1 - 2 * (r & 1)
    first = h == 0

    own_ctx, cot, mom, param = context[0].T, out_grad[0], momentum[0], params[0]
    tokens = own_ctx.shape[1]

    near, far = own_ctx[:, : tokens // 2], own_ctx[:, tokens // 2 :]
    give_ctx = jnp.where(first, far, near)
    own_half = jnp.where(first, near, far)
    oth_half = swapped(give_ctx)
    cot, give_ctx = tied(cot, give_ctx)

    a0 = cot[:, CUTS[0][0] : CUTS[0][1]]
    b0 = cot[:, CUTS[1][0] : CUTS[1][1]]
    a1 = ring_step(a0)
    param, a0, b0 = tied(param, a0, b0)
    p16 = param.astype(bf16)
    p16, oth_half, a1 = tied(p16, oth_half, a1)
    p_low, p_up = passed_along(p16, 1), passed_along(p16, -1)
    a2 = ring_step(a1)
    b0, a2, a0 = tied(b0, a2, a0)
    p_low, p_up, a2 = tied(p_low, p_up, a2)

    p1 = third(param, p_low, p_up)
    p1_16 = p1.astype(bf16)
    p2_low, p2_up = passed_along(p1_16, 2), passed_along(p1_16, -2)
    a3 = ring_step(a2)
    b1 = ring_step(b0)

    spots = [(y - way * step) & 3 for step in range(4)]

    def in_ring_order(value):
        blocks = [value[:, 256 * k : 256 * k + 256] for k in range(4)]
        return [
            jnp.where(s < 2, jnp.where(s == 0, blocks[0], blocks[1]), jnp.where(s == 2, blocks[2], blocks[3])) for s in spots
        ]

    def gradient(blocks):
        own, oth = None, None
        for step in range(4):
            a = jnp.dot(own_by_step[step], blocks[step], preferred_element_type=f32)
            b = jnp.dot(oth_by_step[step], blocks[step], preferred_element_type=f32)
            own, oth = (a, b) if step == 0 else (own + a, oth + b)
        return own, oth.astype(bf16)

    b2 = ring_step(b1)
    own_by_step, oth_by_step = in_ring_order(own_half), in_ring_order(oth_half)
    own_a, give_a = gradient((a0, a1, a2, a3))
    back_a = swapped(give_a)
    b2, give_a = tied(b2, give_a)
    b3 = ring_step(b2)

    own_b, give_b = gradient((b0, b1, b2, b3))
    back_b = swapped(give_b)
    back_a, p2_low, p2_up, give_b = tied(back_a, p2_low, p2_up, give_b)
    p_mixed = third(p1, p2_low, p2_up)

    v_a = beta_decay * mom[:, CUTS[0][0] : CUTS[0][1]].astype(f32) + own_a + back_a.astype(f32)
    va16 = v_a.astype(bf16)
    va_low, va_up = passed_along(va16, 1), passed_along(va16, -1)
    v_b = beta_decay * mom[:, CUTS[1][0] : CUTS[1][1]].astype(f32) + own_b + back_b.astype(f32)
    vb16 = v_b.astype(bf16)
    vb16, va16 = tied(vb16, va16)
    vb_low, vb_up = passed_along(vb16, 1), passed_along(vb16, -1)

    va_low, va_up, vb16 = tied(va_low, va_up, vb16)
    v1_a = third(v_a, va_low, va_up)
    v1a16 = v1_a.astype(bf16)
    va2_low, va2_up = passed_along(v1a16, 2), passed_along(v1a16, -2)
    vb_low, vb_up, v1a16 = tied(vb_low, vb_up, v1a16)
    v1_b = third(v_b, vb_low, vb_up)
    v1b16 = v1_b.astype(bf16)
    vb2_low, vb2_up = passed_along(v1b16, 2), passed_along(v1b16, -2)

    out_p = p_mixed
    out_m = jnp.zeros(mom.shape, bf16)
    for (lo, hi), v1, low, up in ((CUTS[0], v1_a, va2_low, va2_up), (CUTS[1], v1_b, vb2_low, vb2_up)):
        velocity = third(v1, low, up)
        weights = p_mixed[:, lo:hi] - learn_rate * velocity
        out_p = lax.dynamic_update_slice(out_p, weights, (0, lo))
        out_m = lax.dynamic_update_slice(out_m, velocity.astype(bf16), (0, lo))
    return (out_p[None], out_m[None])


def solution(mesh):
    return jax.shard_map(
        body,
        mesh=mesh,
        in_specs=(
            P("replica", None, "tensor"),
            P("replica", "tensor", None),
            P("replica", "tensor", None),
            P("replica", "tensor", None),
        ),
        out_specs=(P("replica", "tensor", None), P("replica", "tensor", None)),
        check_vma=False,
    )
```

time: 321 us -> 187 us (0.58)
  waiting for transfers between devices: 279 us -> 118 us
  starting transfers between devices: 12.2 us -> 39.4 us
  between operations: 14.1 us -> 0.91 us
  other arithmetic: 5.22 us -> 17.1 us
  local copies, waits for them, and re-layouts: 0.01 us -> 4.02 us
  matrix products: 10.3 us -> 6.86 us
    all_gather x1 -> x0, waiting for transfers between devices: 175 us -> none  [body(): gathered = lax.all_gather(out_grad, 'tensor', axis=1, tiled=True)]
    ppermute x8 -> x21, starting transfers between devices: 12.2 us -> 39.4 us  [the longest x12 19.5 us: passed_along(): return lax.ppermute(value, 'replica', pairs)]
    ppermute x8 -> x21, waiting for transfers between devices: 103 us -> 118 us  [the longest x3 52.2 us: swapped(): return lax.ppermute(value, 'tensor', [(t, t ^ 4) for t in range(8)])]
    select_n x0 -> x5, other arithmetic: none -> 5.59 us  [the longest x4 3.46 us: in_ring_order(): jnp.where(s < 2, jnp.where(s == 0, blocks[0], blocks[1]), jnp.where(s ==...]
    convert_element_type x1 -> x6, other arithmetic: 1.44 us -> 5.79 us  [the longest x1 2.49 us: body(): p1_16 = p1.astype(bf16)]
    dot_general x1 -> x16, matrix products: 10.3 us -> 6.86 us  [the longest x8 3.66 us: gradient(): a = jnp.dot(own_by_step[step], blocks[step], preferred_element_type=f32)]
  transfers between devices with their start and end apart: 9 -> 21, of which waited for: 7 -> 15; matrix products, arithmetic and copies ran while one was open for 0% -> 11% of each run, Pallas kernels for 0% -> 0%
where the time goes in v2:
time: 187 us
  waiting for transfers between devices  118 us (63%)
  starting transfers between devices  39.4 us (21%)
  other arithmetic  17.1 us (9%)
  matrix products  6.86 us (4%)
  local copies, waits for them, and re-layouts  4.02 us (2%)
    ppermute x3, waiting for transfers between devices, swapped(): return lax.ppermute(value, 'tensor', [(t, t ^ 4) for t in range(8)])  52.2 us
    ppermute x12, waiting for transfers between devices, passed_along(): return lax.ppermute(value, 'replica', pairs)  35.4 us
    ppermute x6, waiting for transfers between devices, ring_step(): return lax.ppermute(value, BOTH, pairs)  30.8 us
    ppermute x12, starting transfers between devices, passed_along(): return lax.ppermute(value, 'replica', pairs)  19.5 us
    ppermute x6, starting transfers between devices, ring_step(): return lax.ppermute(value, BOTH, pairs)  11.5 us
    ppermute x3, starting transfers between devices, swapped(): return lax.ppermute(value, 'tensor', [(t, t ^ 4) for t in range(8)])  8.4 us
  transfers between devices with their start and end apart: 21, of which 15 were waited for; matrix products, arithmetic and copies ran while one was open for 11% of the time, Pallas kernels for 0%

profile of v2, /device:TPU:1, one launch (start us, length us, event | category | flops | bytes accessed | tf_op | source)
XLA Modules:
  0.0 186.7 jit_solution(2495451860103876404)
XLA Ops:
  0.6 2.1 %broadcast_select_fusion = (bf16[224,1024]{1,0:T(8,128)(2,1)}, bf16[224,1024]{1,0:T(8,128)(2,1)S(1)}) fusion(pred[]{:T(512)S(6)} %eq.35, bf16[224,2048]{1,0:T(8,128)(2,1)} %bitcast.57), kind=kLoop, calls=%fused_computation.34 | loop fusion | flops 458752 | bytes 1835009 | tf_op jit(solution)/shard_map/jit(_where)/select_n | solution.py:51
  2.9 3.6 %collective-permute-start.1 = (bf16[256,2048]{1,0:T(8,128)(2,1)S(1)}, bf16[256,2048]{1,0:T(8,128)(2,1)S(1)}, u32[]{:S(2)}, u32[]{:S(2)}) collective-permute-start(bf16[256,2048]{1,0:T(8,128)(2,1)S(1)} %slice.50), channel_id=1, source_target_pairs={{0,1},{1,2},{2,3},{3,0},{4,5},{5,6},{6,7},{7,4},{8,11},{9,8},{10,9... | collective-permute-start | bytes 3145736 | tf_op jit(solution)/shard_map/ppermute | solution.py:29
  6.6 2.7 %collective-permute-start = (bf16[224,1024]{1,0:T(8,128)(2,1)S(1)}, bf16[224,1024]{1,0:T(8,128)(2,1)S(1)}, u32[]{:S(2)}, u32[]{:S(2)}) collective-permute-start(bf16[224,1024]{1,0:T(8,128)(2,1)S(1)} %get-tuple-element.47), channel_id=1, source_target_pairs={{0,4},{1,5},{2,6},{3,7},{4,0},{5,1},{6,2},{7,3},{8,12},{9,13},{10,... | collective-permute-start | bytes 1376264 | tf_op jit(solution)/shard_map/ppermute | solution.py:20
  9.3 1.0 slice.51
  10.3 1.3 convert_element_type.78
  11.6 8.8 %collective-permute-done = bf16[224,1024]{1,0:T(8,128)(2,1)S(1)} collective-permute-done((bf16[224,1024]{1,0:T(8,128)(2,1)S(1)}, bf16[224,1024]{1,0:T(8,128)(2,1)S(1)}, u32[]{:S(2)}, u32[]{:S(2)}) %collective-permute-start) | collective-permute-done | bytes 458784 | tf_op jit(solution)/shard_map/ppermute | solution.py:20
  20.4 1.0 copy-done.4
  21.4 2.1 %collective-permute-start.2 = (bf16[224,3584]{1,0:T(8,128)(2,1)}, bf16[224,3584]{1,0:T(8,128)(2,1)}, u32[]{:S(2)}, u32[]{:S(2)}) collective-permute-start(bf16[224,3584]{1,0:T(8,128)(2,1)} %convert_element_type.78), channel_id=1, source_target_pairs={{0,8},{8,16},{16,24},{24,32},{32,40},{40,48},{48,56},{56,64},{64,7... | collective-permute-start | bytes 4816904 | tf_op jit(solution)/shard_map/ppermute | solution.py:16
  23.5 1.2 select_select_fusion.1
  24.7 1.1 select_select_fusion.3
  25.8 1.1 collective-permute-start.4
  26.9 1.1 select_select_fusion.5
  28.9 11.2 %collective-permute-done.4 = bf16[256,2048]{1,0:T(8,128)(2,1)S(1)} collective-permute-done((bf16[256,2048]{1,0:T(8,128)(2,1)}, bf16[256,2048]{1,0:T(8,128)(2,1)S(1)}, u32[]{:S(2)}, u32[]{:S(2)}) %collective-permute-start.4) | collective-permute-done | bytes 1048608 | tf_op jit(solution)/shard_map/ppermute | solution.py:29
  40.2 2.2 %collective-permute-start.9 = (bf16[256,1536]{1,0:T(8,128)(2,1)S(1)}, bf16[256,1536]{1,0:T(8,128)(2,1)S(1)}, u32[]{:S(2)}, u32[]{:S(2)}) collective-permute-start(bf16[256,1536]{1,0:T(8,128)(2,1)S(1)} %copy-done.3), channel_id=1, source_target_pairs={{0,1},{1,2},{2,3},{3,0},{4,5},{5,6},{6,7},{7,4},{8,11},{9,8},{10,9... | collective-permute-start | bytes 2359304 | tf_op jit(solution)/shard_map/ppermute | solution.py:29
  42.4 1.9 %collective-permute-done.3 = bf16[224,3584]{1,0:T(8,128)(2,1)} collective-permute-done((bf16[224,3584]{1,0:T(8,128)(2,1)}, bf16[224,3584]{1,0:T(8,128)(2,1)}, u32[]{:S(2)}, u32[]{:S(2)}) %collective-permute-start.3) | collective-permute-done | bytes 1605664 | tf_op jit(solution)/shard_map/ppermute | solution.py:16
  44.3 1.0 collective-permute-start.5
  45.3 2.5 %fusion.16 = bf16[224,3584]{1,0:T(8,128)(2,1)S(1)} fusion(bf16[224,3584]{1,0:T(8,128)(2,1)} %collective-permute-done.3, f32[224,3584]{1,0:T(8,128)S(1)} %bitcast.50, bf16[224,3584]{1,0:T(8,128)(2,1)} %collective-permute-done.2), kind=kLoop, calls=%fused_computation.33 | loop fusion | flops 4816896 | bytes 8028160 | tf_op jit(solution)/shard_map/convert_element_type | solution.py:67
  47.8 1.4 collective-permute-start.7
  49.2 4.9 %collective-permute-start.8 = (bf16[224,3584]{1,0:T(8,128)(2,1)S(1)}, bf16[224,3584]{1,0:T(8,128)(2,1)S(1)}, u32[]{:S(2)}, u32[]{:S(2)}) collective-permute-start(bf16[224,3584]{1,0:T(8,128)(2,1)S(1)} %fusion.16), channel_id=1, source_target_pairs={{0,240},{8,248},{16,0},{24,8},{32,16},{40,24},{48,32},{56,40},{64,... | collective-permute-start | bytes 4816904 | tf_op jit(solution)/shard_map/ppermute | solution.py:16
  55.5 7.1 %collective-permute-done.5 = bf16[256,2048]{1,0:T(8,128)(2,1)S(1)} collective-permute-done((bf16[256,2048]{1,0:T(8,128)(2,1)S(1)}, bf16[256,2048]{1,0:T(8,128)(2,1)S(1)}, u32[]{:S(2)}, u32[]{:S(2)}) %collective-permute-start.5) | collective-permute-done | bytes 1048608 | tf_op jit(solution)/shard_map/ppermute | solution.py:29
  63.0 0.6 fusion.10
  63.6 7.4 %collective-permute-done.10 = bf16[256,1536]{1,0:T(8,128)(2,1)S(1)} collective-permute-done((bf16[256,1536]{1,0:T(8,128)(2,1)S(1)}, bf16[256,1536]{1,0:T(8,128)(2,1)S(1)}, u32[]{:S(2)}, u32[]{:S(2)}) %collective-permute-start.10) | collective-permute-done | bytes 786464 | tf_op jit(solution)/shard_map/ppermute | solution.py:29
  71.0 3.4 %collective-permute-start.11 = (bf16[256,1536]{1,0:T(8,128)(2,1)S(1)}, bf16[256,1536]{1,0:T(8,128)(2,1)S(1)}, u32[]{:S(2)}, u32[]{:S(2)}) collective-permute-start(bf16[256,1536]{1,0:T(8,128)(2,1)S(1)} %collective-permute-done.10), channel_id=1, source_target_pairs={{0,1},{1,2},{2,3},{3,0},{4,5},{5,6},{6,7},{7,4},{8,11},{9,8},{10,9... | collective-permute-start | bytes 2359304 | tf_op jit(solution)/shard_map/ppermute | solution.py:29
  74.8 2.8 %collective-permute-start.6 = (bf16[224,2048]{1,0:T(8,128)(2,1)S(1)}, bf16[224,2048]{1,0:T(8,128)(2,1)S(1)}, u32[]{:S(2)}, u32[]{:S(2)}) collective-permute-start(bf16[224,2048]{1,0:T(8,128)(2,1)S(1)} %fusion.10), channel_id=1, source_target_pairs={{0,4},{1,5},{2,6},{3,7},{4,0},{5,1},{6,2},{7,3},{8,12},{9,13},{10,... | collective-permute-start | bytes 2752520 | tf_op jit(solution)/shard_map/ppermute | solution.py:20
  78.4 5.0 %collective-permute-done.11 = bf16[256,1536]{1,0:T(8,128)(2,1)S(1)} collective-permute-done((bf16[256,1536]{1,0:T(8,128)(2,1)S(1)}, bf16[256,1536]{1,0:T(8,128)(2,1)S(1)}, u32[]{:S(2)}, u32[]{:S(2)}) %collective-permute-start.11) | collective-permute-done | bytes 786464 | tf_op jit(solution)/shard_map/ppermute | solution.py:29
  84.1 2.8 %collective-permute-start.14 = (bf16[224,1536]{1,0:T(8,128)(2,1)S(1)}, bf16[224,1536]{1,0:T(8,128)(2,1)S(1)}, u32[]{:S(2)}, u32[]{:S(2)}) collective-permute-start(bf16[224,1536]{1,0:T(8,128)(2,1)S(1)} %fusion.11), channel_id=1, source_target_pairs={{0,4},{1,5},{2,6},{3,7},{4,0},{5,1},{6,2},{7,3},{8,12},{9,13},{10,... | collective-permute-start | bytes 2064392 | tf_op jit(solution)/shard_map/ppermute | solution.py:20
  86.9 2.6 %collective-permute-done.7 = bf16[224,3584]{1,0:T(8,128)(2,1)S(1)} collective-permute-done((bf16[224,3584]{1,0:T(8,128)(2,1)S(1)}, bf16[224,3584]{1,0:T(8,128)(2,1)S(1)}, u32[]{:S(2)}, u32[]{:S(2)}) %collective-permute-start.7) | collective-permute-done | bytes 1605664 | tf_op jit(solution)/shard_map/ppermute | solution.py:16
  89.5 21.2 %collective-permute-done.6 = bf16[224,2048]{1,0:T(8,128)(2,1)S(1)} collective-permute-done((bf16[224,2048]{1,0:T(8,128)(2,1)S(1)}, bf16[224,2048]{1,0:T(8,128)(2,1)S(1)}, u32[]{:S(2)}, u32[]{:S(2)}) %collective-permute-start.6) | collective-permute-done | bytes 917536 | tf_op jit(solution)/shard_map/ppermute | solution.py:20
  110.7 0.9 fusion.19
  111.7 0.7 collective-permute-start.13
  113.0 22.2 %collective-permute-done.14 = bf16[224,1536]{1,0:T(8,128)(2,1)S(1)} collective-permute-done((bf16[224,1536]{1,0:T(8,128)(2,1)S(1)}, bf16[224,1536]{1,0:T(8,128)(2,1)S(1)}, u32[]{:S(2)}, u32[]{:S(2)}) %collective-permute-start.14) | collective-permute-done | bytes 688160 | tf_op jit(solution)/shard_map/ppermute | solution.py:20
  135.3 0.5 fusion.20
  135.9 0.6 collective-permute-start.18
  136.5 0.4 fusion.18
  136.9 3.5 %collective-permute-start.16 = (bf16[224,2048]{1,0:T(8,128)(2,1)S(1)}, bf16[224,2048]{1,0:T(8,128)(2,1)S(1)}, u32[]{:S(2)}, u32[]{:S(2)}) collective-permute-start(bf16[224,2048]{1,0:T(8,128)(2,1)S(1)} %fusion.18), channel_id=1, source_target_pairs={{0,240},{8,248},{16,0},{24,8},{32,16},{40,24},{48,32},{56,40},{64,... | collective-permute-start | bytes 2752520 | tf_op jit(solution)/shard_map/ppermute | solution.py:16
  140.4 3.1 %add_multiply_fusion = f32[224,3584]{1,0:T(8,128)S(1)} fusion(bf16[224,3584]{1,0:T(8,128)(2,1)S(1)} %collective-permute-done.8, bf16[224,3584]{1,0:T(8,128)(2,1)S(1)} %collective-permute-done.7, bf16[224,3584]{1,0:T(8,128)(2,1)} %collective-permute-done.3, f32[224,3584]{1,0:T(8,128)S(1)} %bitcast.51, bf16[224,3584]{1,0:T(8,128)(2,1)} %collective-permute-done.2), kind=kLoop, calls=%fused_computation | loop fusion | flops 8028160 | bytes 12845056 | tf_op jit(solution)/shard_map/div | solution.py:37
  144.0 9.6 %collective-permute-done.18 = bf16[224,1536]{1,0:T(8,128)(2,1)S(1)} collective-permute-done((bf16[224,1536]{1,0:T(8,128)(2,1)S(1)}, bf16[224,1536]{1,0:T(8,128)(2,1)S(1)}, u32[]{:S(2)}, u32[]{:S(2)}) %collective-permute-start.18) | collective-permute-done | bytes 688160 | tf_op jit(solution)/shard_map/ppermute | solution.py:16
  153.9 6.1 %collective-permute-start.20 = (bf16[224,1536]{1,0:T(8,128)(2,1)S(1)}, bf16[224,1536]{1,0:T(8,128)(2,1)S(1)}, u32[]{:S(2)}, u32[]{:S(2)}) collective-permute-start(bf16[224,1536]{1,0:T(8,128)(2,1)S(1)} %fusion.17), channel_id=1, source_target_pairs={{0,240},{8,248},{16,0},{24,8},{32,16},{40,24},{48,32},{56,40},{64,... | collective-permute-start | bytes 2064392 | tf_op jit(solution)/shard_map/ppermute | solution.py:16
  160.0 0.5 collective-permute-done.16
  160.5 8.6 %collective-permute-done.15 = bf16[224,2048]{1,0:T(8,128)(2,1)S(1)} collective-permute-done((bf16[224,2048]{1,0:T(8,128)(2,1)S(1)}, bf16[224,2048]{1,0:T(8,128)(2,1)S(1)}, u32[]{:S(2)}, u32[]{:S(2)}) %collective-permute-start.15) | collective-permute-done | bytes 917536 | tf_op jit(solution)/shard_map/ppermute | solution.py:16
  169.1 0.8 multiply_convert_fusion
  169.9 0.8 fusion.13
  170.7 4.7 %collective-permute-done.20 = bf16[224,1536]{1,0:T(8,128)(2,1)S(1)} collective-permute-done((bf16[224,1536]{1,0:T(8,128)(2,1)S(1)}, bf16[224,1536]{1,0:T(8,128)(2,1)S(1)}, u32[]{:S(2)}, u32[]{:S(2)}) %collective-permute-start.20) | collective-permute-done | bytes 688160 | tf_op jit(solution)/shard_map/ppermute | solution.py:16
  175.4 7.2 %collective-permute-done.19 = bf16[224,1536]{1,0:T(8,128)(2,1)S(1)} collective-permute-done((bf16[224,1536]{1,0:T(8,128)(2,1)S(1)}, bf16[224,1536]{1,0:T(8,128)(2,1)S(1)}, u32[]{:S(2)}, u32[]{:S(2)}) %collective-permute-start.19) | collective-permute-done | bytes 688160 | tf_op jit(solution)/shard_map/ppermute | solution.py:16
  182.6 0.5 multiply_convert_fusion.1
  183.1 1.3 maximum_bitcast_fusion
  184.4 0.6 fusion.15
  185.0 1.7 copy-done.6
  (50 shorter events, 6.1 us)
Async XLA Ops:
  0.6 2.1 %copy-start.7 = (bf16[1,256,3584]{2,1,0:T(8,128)(2,1)S(1)}, bf16[1,256,3584]{2,1,0:T(8,128)(2,1)}, u32[]{:S(2)}) copy-start(bf16[1,256,3584]{2,1,0:T(8,128)(2,1)} %param.5) | copy-start | bytes 5505028
  2.8 7.5 %copy-start = (f32[1,224,3584]{2,1,0:T(8,128)S(1)}, f32[1,224,3584]{2,1,0:T(8,128)}, u32[]{:S(2)}) copy-start(f32[1,224,3584]{2,1,0:T(8,128)} %param.6) | copy-start | bytes 9633796
  2.9 8.7 %copy-start.1 = (bf16[256,2048]{1,0:T(8,128)(2,1)}, bf16[256,2048]{1,0:T(8,128)(2,1)S(1)}, u32[]{:S(2)}) copy-start(bf16[256,2048]{1,0:T(8,128)(2,1)S(1)} %slice.50) | copy-start | bytes 3145732
  2.9 17.4 %collective-permute-start.1 = (bf16[256,2048]{1,0:T(8,128)(2,1)S(1)}, bf16[256,2048]{1,0:T(8,128)(2,1)S(1)}, u32[]{:S(2)}, u32[]{:S(2)}) collective-permute-start(bf16[256,2048]{1,0:T(8,128)(2,1)S(1)} %slice.50), channel_id=1, source_target_pairs={{0,1},{1,2},{2,3},{3,0},{4,5},{5,6},{6,7},{7,4},{8,11},{9,8},{10,9... | collective-permute-start | bytes 3145736 | tf_op jit(solution)/shard_map/ppermute | solution.py:29
  6.6 13.8 %collective-permute-start = (bf16[224,1024]{1,0:T(8,128)(2,1)S(1)}, bf16[224,1024]{1,0:T(8,128)(2,1)S(1)}, u32[]{:S(2)}, u32[]{:S(2)}) collective-permute-start(bf16[224,1024]{1,0:T(8,128)(2,1)S(1)} %get-tuple-element.47), channel_id=1, source_target_pairs={{0,4},{1,5},{2,6},{3,7},{4,0},{5,1},{6,2},{7,3},{8,12},{9,13},{10,... | collective-permute-start | bytes 1376264 | tf_op jit(solution)/shard_map/ppermute | solution.py:20
  20.4 3.1 %copy-start.8 = (bf16[224,1024]{1,0:T(8,128)(2,1)}, bf16[224,1024]{1,0:T(8,128)(2,1)S(1)}, u32[]{:S(2)}) copy-start(bf16[224,1024]{1,0:T(8,128)(2,1)S(1)} %collective-permute-done) | copy-start | bytes 1376260
  20.4 1.0 copy-start.4
  21.4 21.0 %collective-permute-start.2 = (bf16[224,3584]{1,0:T(8,128)(2,1)}, bf16[224,3584]{1,0:T(8,128)(2,1)}, u32[]{:S(2)}, u32[]{:S(2)}) collective-permute-start(bf16[224,3584]{1,0:T(8,128)(2,1)} %convert_element_type.78), channel_id=1, source_target_pairs={{0,8},{8,16},{16,24},{24,32},{32,40},{40,48},{48,56},{56,64},{64,7... | collective-permute-start | bytes 4816904 | tf_op jit(solution)/shard_map/ppermute | solution.py:16
  23.5 20.8 %collective-permute-start.3 = (bf16[224,3584]{1,0:T(8,128)(2,1)}, bf16[224,3584]{1,0:T(8,128)(2,1)}, u32[]{:S(2)}, u32[]{:S(2)}) collective-permute-start(bf16[224,3584]{1,0:T(8,128)(2,1)} %convert_element_type.78), channel_id=1, source_target_pairs={{0,248},{8,0},{16,8},{24,16},{32,24},{40,32},{48,40},{56,48},{64,5... | collective-permute-start | bytes 4816904 | tf_op jit(solution)/shard_map/ppermute | solution.py:16
  23.5 4.5 %copy-start.9 = (bf16[224,1024]{1,0:T(8,128)(2,1)S(1)}, bf16[224,1024]{1,0:T(8,128)(2,1)}, u32[]{:S(2)}) copy-start(bf16[224,1024]{1,0:T(8,128)(2,1)} %copy-done.8) | copy-start | bytes 1376260
  23.5 4.6 %copy-start.5 = (bf16[256,2048]{1,0:T(8,128)(2,1)S(1)}, bf16[256,2048]{1,0:T(8,128)(2,1)}, u32[]{:S(2)}) copy-start(bf16[256,2048]{1,0:T(8,128)(2,1)} %copy-done.4) | copy-start | bytes 3145732
  25.8 14.3 %collective-permute-start.4 = (bf16[256,2048]{1,0:T(8,128)(2,1)}, bf16[256,2048]{1,0:T(8,128)(2,1)S(1)}, u32[]{:S(2)}, u32[]{:S(2)}) collective-permute-start(bf16[256,2048]{1,0:T(8,128)(2,1)} %copy-done.4), channel_id=1, source_target_pairs={{0,1},{1,2},{2,3},{3,0},{4,5},{5,6},{6,7},{7,4},{8,11},{9,8},{10,9... | collective-permute-start | bytes 3145736 | tf_op jit(solution)/shard_map/ppermute | solution.py:29
  28.5 11.7 %copy-start.3 = (bf16[256,1536]{1,0:T(8,128)(2,1)S(1)}, bf16[256,1536]{1,0:T(8,128)(2,1)}, u32[]{:S(2)}) copy-start(bf16[256,1536]{1,0:T(8,128)(2,1)} %slice.51) | copy-start | bytes 2359300
  40.2 14.8 %collective-permute-start.9 = (bf16[256,1536]{1,0:T(8,128)(2,1)S(1)}, bf16[256,1536]{1,0:T(8,128)(2,1)S(1)}, u32[]{:S(2)}, u32[]{:S(2)}) collective-permute-start(bf16[256,1536]{1,0:T(8,128)(2,1)S(1)} %copy-done.3), channel_id=1, source_target_pairs={{0,1},{1,2},{2,3},{3,0},{4,5},{5,6},{6,7},{7,4},{8,11},{9,8},{10,9... | collective-permute-start | bytes 2359304 | tf_op jit(solution)/shard_map/ppermute | solution.py:29
  44.3 18.3 %collective-permute-start.5 = (bf16[256,2048]{1,0:T(8,128)(2,1)S(1)}, bf16[256,2048]{1,0:T(8,128)(2,1)S(1)}, u32[]{:S(2)}, u32[]{:S(2)}) collective-permute-start(bf16[256,2048]{1,0:T(8,128)(2,1)S(1)} %collective-permute-done.4), channel_id=1, source_target_pairs={{0,1},{1,2},{2,3},{3,0},{4,5},{5,6},{6,7},{7,4},{8,11},{9,8},{10,9... | collective-permute-start | bytes 3145736 | tf_op jit(solution)/shard_map/ppermute | solution.py:29
  47.8 41.7 %collective-permute-start.7 = (bf16[224,3584]{1,0:T(8,128)(2,1)S(1)}, bf16[224,3584]{1,0:T(8,128)(2,1)S(1)}, u32[]{:S(2)}, u32[]{:S(2)}) collective-permute-start(bf16[224,3584]{1,0:T(8,128)(2,1)S(1)} %fusion.16), channel_id=1, source_target_pairs={{0,16},{8,24},{16,32},{24,40},{32,48},{40,56},{48,64},{56,72},{64,... | collective-permute-start | bytes 4816904 | tf_op jit(solution)/shard_map/ppermute | solution.py:16
  49.2 40.3 %collective-permute-start.8 = (bf16[224,3584]{1,0:T(8,128)(2,1)S(1)}, bf16[224,3584]{1,0:T(8,128)(2,1)S(1)}, u32[]{:S(2)}, u32[]{:S(2)}) collective-permute-start(bf16[224,3584]{1,0:T(8,128)(2,1)S(1)} %fusion.16), channel_id=1, source_target_pairs={{0,240},{8,248},{16,0},{24,8},{32,16},{40,24},{48,32},{56,40},{64,... | collective-permute-start | bytes 4816904 | tf_op jit(solution)/shard_map/ppermute | solution.py:16
  55.0 16.0 %collective-permute-start.10 = (bf16[256,1536]{1,0:T(8,128)(2,1)S(1)}, bf16[256,1536]{1,0:T(8,128)(2,1)S(1)}, u32[]{:S(2)}, u32[]{:S(2)}) collective-permute-start(bf16[256,1536]{1,0:T(8,128)(2,1)S(1)} %collective-permute-done.9), channel_id=1, source_target_pairs={{0,1},{1,2},{2,3},{3,0},{4,5},{5,6},{6,7},{7,4},{8,11},{9,8},{10,9... | collective-permute-start | bytes 2359304 | tf_op jit(solution)/shard_map/ppermute | solution.py:29
  55.4 7.6 %copy-start.2 = (bf16[256,2048]{1,0:T(8,128)(2,1)S(1)}, bf16[256,2048]{1,0:T(8,128)(2,1)}, u32[]{:S(2)}) copy-start(bf16[256,2048]{1,0:T(8,128)(2,1)} %copy-done.1) | copy-start | bytes 3145732
  71.0 12.3 %collective-permute-start.11 = (bf16[256,1536]{1,0:T(8,128)(2,1)S(1)}, bf16[256,1536]{1,0:T(8,128)(2,1)S(1)}, u32[]{:S(2)}, u32[]{:S(2)}) collective-permute-start(bf16[256,1536]{1,0:T(8,128)(2,1)S(1)} %collective-permute-done.10), channel_id=1, source_target_pairs={{0,1},{1,2},{2,3},{3,0},{4,5},{5,6},{6,7},{7,4},{8,11},{9,8},{10,9... | collective-permute-start | bytes 2359304 | tf_op jit(solution)/shard_map/ppermute | solution.py:29
  74.8 35.9 %collective-permute-start.6 = (bf16[224,2048]{1,0:T(8,128)(2,1)S(1)}, bf16[224,2048]{1,0:T(8,128)(2,1)S(1)}, u32[]{:S(2)}, u32[]{:S(2)}) collective-permute-start(bf16[224,2048]{1,0:T(8,128)(2,1)S(1)} %fusion.10), channel_id=1, source_target_pairs={{0,4},{1,5},{2,6},{3,7},{4,0},{5,1},{6,2},{7,3},{8,12},{9,13},{10,... | collective-permute-start | bytes 2752520 | tf_op jit(solution)/shard_map/ppermute | solution.py:20
  83.7 27.0 %copy-start.10 = (bf16[1,224,3584]{2,1,0:T(8,128)(2,1)S(1)}, bf16[1,224,3584]{2,1,0:T(8,128)(2,1)}, u32[]{:S(2)}) copy-start(bf16[1,224,3584]{2,1,0:T(8,128)(2,1)} %param.7) | copy-start | bytes 4816900
  84.1 51.2 %collective-permute-start.14 = (bf16[224,1536]{1,0:T(8,128)(2,1)S(1)}, bf16[224,1536]{1,0:T(8,128)(2,1)S(1)}, u32[]{:S(2)}, u32[]{:S(2)}) collective-permute-start(bf16[224,1536]{1,0:T(8,128)(2,1)S(1)} %fusion.11), channel_id=1, source_target_pairs={{0,4},{1,5},{2,6},{3,7},{4,0},{5,1},{6,2},{7,3},{8,12},{9,13},{10,... | collective-permute-start | bytes 2064392 | tf_op jit(solution)/shard_map/ppermute | solution.py:20
  111.6 24.9 %collective-permute-start.12 = (bf16[224,2048]{1,0:T(8,128)(2,1)S(1)}, bf16[224,2048]{1,0:T(8,128)(2,1)S(1)}, u32[]{:S(2)}, u32[]{:S(2)}) collective-permute-start(bf16[224,2048]{1,0:T(8,128)(2,1)S(1)} %get-tuple-element.56), channel_id=1, source_target_pairs={{0,8},{8,16},{16,24},{24,32},{32,40},{40,48},{48,56},{56,64},{64,7... | collective-permute-start | bytes 2752520 | tf_op jit(solution)/shard_map/ppermute | solution.py:16
  111.7 24.8 %collective-permute-start.13 = (bf16[224,2048]{1,0:T(8,128)(2,1)S(1)}, bf16[224,2048]{1,0:T(8,128)(2,1)S(1)}, u32[]{:S(2)}, u32[]{:S(2)}) collective-permute-start(bf16[224,2048]{1,0:T(8,128)(2,1)S(1)} %get-tuple-element.56), channel_id=1, source_target_pairs={{0,248},{8,0},{16,8},{24,16},{32,24},{40,32},{48,40},{56,48},{64,5... | collective-permute-start | bytes 2752520 | tf_op jit(solution)/shard_map/ppermute | solution.py:16
  135.8 8.2 %collective-permute-start.17 = (bf16[224,1536]{1,0:T(8,128)(2,1)S(1)}, bf16[224,1536]{1,0:T(8,128)(2,1)S(1)}, u32[]{:S(2)}, u32[]{:S(2)}) collective-permute-start(bf16[224,1536]{1,0:T(8,128)(2,1)S(1)} %get-tuple-element.41), channel_id=1, source_target_pairs={{0,8},{8,16},{16,24},{24,32},{32,40},{40,48},{48,56},{56,64},{64,7... | collective-permute-start | bytes 2064392 | tf_op jit(solution)/shard_map/ppermute | solution.py:16
  135.9 17.7 %collective-permute-start.18 = (bf16[224,1536]{1,0:T(8,128)(2,1)S(1)}, bf16[224,1536]{1,0:T(8,128)(2,1)S(1)}, u32[]{:S(2)}, u32[]{:S(2)}) collective-permute-start(bf16[224,1536]{1,0:T(8,128)(2,1)S(1)} %get-tuple-element.41), channel_id=1, source_target_pairs={{0,248},{8,0},{16,8},{24,16},{32,24},{40,32},{48,40},{56,48},{64,5... | collective-permute-start | bytes 2064392 | tf_op jit(solution)/shard_map/ppermute | solution.py:16
  136.9 23.6 %collective-permute-start.16 = (bf16[224,2048]{1,0:T(8,128)(2,1)S(1)}, bf16[224,2048]{1,0:T(8,128)(2,1)S(1)}, u32[]{:S(2)}, u32[]{:S(2)}) collective-permute-start(bf16[224,2048]{1,0:T(8,128)(2,1)S(1)} %fusion.18), channel_id=1, source_target_pairs={{0,240},{8,248},{16,0},{24,8},{32,16},{40,24},{48,32},{56,40},{64,... | collective-permute-start | bytes 2752520 | tf_op jit(solution)/shard_map/ppermute | solution.py:16
  140.4 28.7 %collective-permute-start.15 = (bf16[224,2048]{1,0:T(8,128)(2,1)S(1)}, bf16[224,2048]{1,0:T(8,128)(2,1)S(1)}, u32[]{:S(2)}, u32[]{:S(2)}) collective-permute-start(bf16[224,2048]{1,0:T(8,128)(2,1)S(1)} %fusion.18), channel_id=1, source_target_pairs={{0,16},{8,24},{16,32},{24,40},{32,48},{40,56},{48,64},{56,72},{64,... | collective-permute-start | bytes 2752520 | tf_op jit(solution)/shard_map/ppermute | solution.py:16
  153.9 21.4 %collective-permute-start.20 = (bf16[224,1536]{1,0:T(8,128)(2,1)S(1)}, bf16[224,1536]{1,0:T(8,128)(2,1)S(1)}, u32[]{:S(2)}, u32[]{:S(2)}) collective-permute-start(bf16[224,1536]{1,0:T(8,128)(2,1)S(1)} %fusion.17), channel_id=1, source_target_pairs={{0,240},{8,248},{16,0},{24,8},{32,16},{40,24},{48,32},{56,40},{64,... | collective-permute-start | bytes 2064392 | tf_op jit(solution)/shard_map/ppermute | solution.py:16
  160.0 22.5 %collective-permute-start.19 = (bf16[224,1536]{1,0:T(8,128)(2,1)S(1)}, bf16[224,1536]{1,0:T(8,128)(2,1)S(1)}, u32[]{:S(2)}, u32[]{:S(2)}) collective-permute-start(bf16[224,1536]{1,0:T(8,128)(2,1)S(1)} %fusion.17), channel_id=1, source_target_pairs={{0,16},{8,24},{16,32},{24,40},{32,48},{40,56},{48,64},{56,72},{64,... | collective-permute-start | bytes 2064392 | tf_op jit(solution)/shard_map/ppermute | solution.py:16
  185.0 1.7 copy-start.6

commit v3 on v2

--- a/solution.py
+++ b/solution.py
@@ -46,6 +46,10 @@
     own_ctx, cot, mom, param = context[0].T, out_grad[0], momentum[0], params[0]
     tokens = own_ctx.shape[1]
 
+    p16 = param.astype(bf16)
+    p_low, p_up = passed_along(p16, 1), passed_along(p16, -1)
+
+    own_ctx, p16 = tied(own_ctx, p16)
     near, far = own_ctx[:, : tokens // 2], own_ctx[:, tokens // 2 :]
     give_ctx = jnp.where(first, far, near)
     own_half = jnp.where(first, near, far)
@@ -55,19 +59,17 @@
     a0 = cot[:, CUTS[0][0] : CUTS[0][1]]
     b0 = cot[:, CUTS[1][0] : CUTS[1][1]]
     a1 = ring_step(a0)
-    param, a0, b0 = tied(param, a0, b0)
-    p16 = param.astype(bf16)
-    p16, oth_half, a1 = tied(p16, oth_half, a1)
-    p_low, p_up = passed_along(p16, 1), passed_along(p16, -1)
+    b0, a1 = tied(b0, a1)
+    b1 = ring_step(b0)
     a2 = ring_step(a1)
-    b0, a2, a0 = tied(b0, a2, a0)
-    p_low, p_up, a2 = tied(p_low, p_up, a2)
 
+    p_low, p_up, a1 = tied(p_low, p_up, a1)
     p1 = third(param, p_low, p_up)
     p1_16 = p1.astype(bf16)
+    p1_16, oth_half = tied(p1_16, oth_half)
     p2_low, p2_up = passed_along(p1_16, 2), passed_along(p1_16, -2)
+    a2, p1_16 = tied(a2, p1_16)
     a3 = ring_step(a2)
-    b1 = ring_step(b0)
 
     spots = [(y - way * step) & 3 for step in range(4)]
 

time: 187 us -> 177 us (0.947)
  waiting for transfers between devices: 118 us -> 108 us
  matrix products: 6.86 us -> 9.2 us
    ppermute x12, waiting for transfers between devices: 35.4 us -> 31 us  [passed_along(): return lax.ppermute(value, 'replica', pairs)]
    select_n x4, other arithmetic: 3.46 us -> 0.13 us  [in_ring_order(): jnp.where(s < 2, jnp.where(s == 0, blocks[0], blocks[1]), jnp.where(s ==...]
    ppermute x3, waiting for transfers between devices: 52.2 us -> 48.9 us  [swapped(): return lax.ppermute(value, 'tensor', [(t, t ^ 4) for t in range(8)])]
    ppermute x6, waiting for transfers between devices: 30.8 us -> 28.6 us  [ring_step(): return lax.ppermute(value, BOTH, pairs)]
    convert_element_type x1, other arithmetic: 1.31 us -> 3.22 us  [body(): p16 = param.astype(bf16)]
  transfers between devices with their start and end apart: 21 -> 21, of which waited for: 15 -> 13; matrix products, arithmetic and copies ran while one was open for 11% -> 12% of each run, Pallas kernels for 0% -> 0%
where the time goes in v3:
time: 177 us
  waiting for transfers between devices  108 us (61%)
  starting transfers between devices  39.3 us (22%)
  other arithmetic  15.7 us (9%)
  matrix products  9.2 us (5%)
  local copies, waits for them, and re-layouts  3.07 us (2%)
    ppermute x3, waiting for transfers between devices, swapped(): return lax.ppermute(value, 'tensor', [(t, t ^ 4) for t in range(8)])  48.9 us
    ppermute x12, waiting for transfers between devices, passed_along(): return lax.ppermute(value, 'replica', pairs)  31 us
    ppermute x6, waiting for transfers between devices, ring_step(): return lax.ppermute(value, BOTH, pairs)  28.6 us
    ppermute x12, starting transfers between devices, passed_along(): return lax.ppermute(value, 'replica', pairs)  17.8 us
    ppermute x6, starting transfers between devices, ring_step(): return lax.ppermute(value, BOTH, pairs)  12.9 us
    ppermute x3, starting transfers between devices, swapped(): return lax.ppermute(value, 'tensor', [(t, t ^ 4) for t in range(8)])  8.58 us
    dot_general x8, matrix products, gradient(): a = jnp.dot(own_by_step[step], blocks[step], preferred_element_type=f32)  4.85 us
    dot_general x8, matrix products, gradient(): b = jnp.dot(oth_by_step[step], blocks[step], preferred_element_type=f32)  4.35 us
  transfers between devices with their start and end apart: 21, of which 13 were waited for; matrix products, arithmetic and copies ran while one was open for 12% of the time, Pallas kernels for 0%

profile of v3, /device:TPU:1, one launch (start us, length us, event | category | flops | bytes accessed | tf_op | source)
XLA Modules:
  0.0 176.5 jit_solution(15887765011835381211)
XLA Ops:
  0.6 3.2 %bitcast_convert_fusion = bf16[224,3584]{1,0:T(8,128)(2,1)} fusion(f32[1,224,3584]{2,1,0:T(8,128)} %param.6), kind=kLoop, calls=%fused_computation.1 | loop fusion | flops 802816 | bytes 4816896 | tf_op jit(solution)/shard_map/convert_element_type | solution.py:49
  3.9 3.0 %collective-permute-start = (bf16[224,3584]{1,0:T(8,128)(2,1)}, bf16[224,3584]{1,0:T(8,128)(2,1)}, u32[]{:S(2)}, u32[]{:S(2)}) collective-permute-start(bf16[224,3584]{1,0:T(8,128)(2,1)} %bitcast_convert_fusion), channel_id=1, source_target_pairs={{0,8},{8,16},{16,24},{24,32},{32,40},{40,48},{48,56},{56,64},{64,7... | collective-permute-start | bytes 4816904 | tf_op jit(solution)/shard_map/ppermute | solution.py:16
  7.1 2.0 %broadcast_select_fusion = (bf16[224,1024]{1,0:T(8,128)(2,1)S(1)}, bf16[224,1024]{1,0:T(8,128)(2,1)}) fusion(pred[]{:T(512)S(6)} %eq.35, bf16[224,2048]{1,0:T(8,128)(2,1)} %bitcast.64), kind=kLoop, calls=%fused_computation.37 | loop fusion | flops 458752 | bytes 1835009 | tf_op jit(solution)/shard_map/jit(_where)/select_n | solution.py:55
  9.1 1.1 slice.51
  10.2 2.5 %collective-permute-start.2 = (bf16[256,2048]{1,0:T(8,128)(2,1)}, bf16[256,2048]{1,0:T(8,128)(2,1)}, u32[]{:S(2)}, u32[]{:S(2)}) collective-permute-start(bf16[256,2048]{1,0:T(8,128)(2,1)} %slice.51), channel_id=1, source_target_pairs={{0,1},{1,2},{2,3},{3,0},{4,5},{5,6},{6,7},{7,4},{8,11},{9,8},{10,9... | collective-permute-start | bytes 3145736 | tf_op jit(solution)/shard_map/ppermute | solution.py:29
  12.8 2.7 %collective-permute-start.3 = (bf16[224,1024]{1,0:T(8,128)(2,1)}, bf16[224,1024]{1,0:T(8,128)(2,1)S(1)}, u32[]{:S(2)}, u32[]{:S(2)}) collective-permute-start(bf16[224,1024]{1,0:T(8,128)(2,1)} %get-tuple-element.41), channel_id=1, source_target_pairs={{0,4},{1,5},{2,6},{3,7},{4,0},{5,1},{6,2},{7,3},{8,12},{9,13},{10,... | collective-permute-start | bytes 1376264 | tf_op jit(solution)/shard_map/ppermute | solution.py:20
  15.7 0.4 fusion.17
  16.1 8.7 %collective-permute-done.2 = bf16[256,2048]{1,0:T(8,128)(2,1)} collective-permute-done((bf16[256,2048]{1,0:T(8,128)(2,1)}, bf16[256,2048]{1,0:T(8,128)(2,1)}, u32[]{:S(2)}, u32[]{:S(2)}) %collective-permute-start.2) | collective-permute-done | bytes 1048608 | tf_op jit(solution)/shard_map/ppermute | solution.py:29
  24.8 3.4 %collective-permute-start.4 = (bf16[256,2048]{1,0:T(8,128)(2,1)}, bf16[256,2048]{1,0:T(8,128)(2,1)S(1)}, u32[]{:S(2)}, u32[]{:S(2)}) collective-permute-start(bf16[256,2048]{1,0:T(8,128)(2,1)} %collective-permute-done.2), channel_id=1, source_target_pairs={{0,1},{1,2},{2,3},{3,0},{4,5},{5,6},{6,7},{7,4},{8,11},{9,8},{10,9... | collective-permute-start | bytes 3145736 | tf_op jit(solution)/shard_map/ppermute | solution.py:29
  28.3 2.6 %fusion.16 = bf16[224,3584]{1,0:T(8,128)(2,1)S(1)} fusion(bf16[224,3584]{1,0:T(8,128)(2,1)} %collective-permute-done.1, bf16[224,3584]{1,0:T(8,128)(2,1)} %collective-permute-done, f32[1,224,3584]{2,1,0:T(8,128)S(1)} %copy-done), kind=kLoop, calls=%fused_computation.36 | loop fusion | flops 4816896 | bytes 8028160 | tf_op jit(solution)/shard_map/convert_element_type | solution.py:68
  30.8 10.3 %collective-permute-done.3 = bf16[224,1024]{1,0:T(8,128)(2,1)S(1)} collective-permute-done((bf16[224,1024]{1,0:T(8,128)(2,1)}, bf16[224,1024]{1,0:T(8,128)(2,1)S(1)}, u32[]{:S(2)}, u32[]{:S(2)}) %collective-permute-start.3) | collective-permute-done | bytes 458784 | tf_op jit(solution)/shard_map/ppermute | solution.py:20
  41.1 3.6 %collective-permute-start.8 = (bf16[224,3584]{1,0:T(8,128)(2,1)S(1)}, bf16[224,3584]{1,0:T(8,128)(2,1)S(1)}, u32[]{:S(2)}, u32[]{:S(2)}) collective-permute-start(bf16[224,3584]{1,0:T(8,128)(2,1)S(1)} %fusion.16), channel_id=1, source_target_pairs={{0,240},{8,248},{16,0},{24,8},{32,16},{40,24},{48,32},{56,40},{64,... | collective-permute-start | bytes 4816904 | tf_op jit(solution)/shard_map/ppermute | solution.py:16
  44.7 0.4 fusion.19
  45.1 2.8 %collective-permute-start.5 = (bf16[256,2048]{1,0:T(8,128)(2,1)S(1)}, bf16[256,2048]{1,0:T(8,128)(2,1)S(1)}, u32[]{:S(2)}, u32[]{:S(2)}) collective-permute-start(bf16[256,2048]{1,0:T(8,128)(2,1)S(1)} %collective-permute-done.4), channel_id=1, source_target_pairs={{0,1},{1,2},{2,3},{3,0},{4,5},{5,6},{6,7},{7,4},{8,11},{9,8},{10,9... | collective-permute-start | bytes 3145736 | tf_op jit(solution)/shard_map/ppermute | solution.py:29
  48.0 1.6 convolution_add_fusion.7
  49.6 1.7 convolution_add_fusion.5
  51.3 0.7 collective-permute-start.10
  52.4 7.5 %collective-permute-done.5 = bf16[256,2048]{1,0:T(8,128)(2,1)S(1)} collective-permute-done((bf16[256,2048]{1,0:T(8,128)(2,1)S(1)}, bf16[256,2048]{1,0:T(8,128)(2,1)S(1)}, u32[]{:S(2)}, u32[]{:S(2)}) %collective-permute-start.5) | collective-permute-done | bytes 1048608 | tf_op jit(solution)/shard_map/ppermute | solution.py:29
  59.8 0.4 fusion.25
  60.2 0.5 fusion.10
  60.7 7.5 %collective-permute-done.10 = bf16[256,1536]{1,0:T(8,128)(2,1)S(1)} collective-permute-done((bf16[256,1536]{1,0:T(8,128)(2,1)S(1)}, bf16[256,1536]{1,0:T(8,128)(2,1)S(1)}, u32[]{:S(2)}, u32[]{:S(2)}) %collective-permute-start.10) | collective-permute-done | bytes 786464 | tf_op jit(solution)/shard_map/ppermute | solution.py:29
  68.3 3.4 %collective-permute-start.11 = (bf16[256,1536]{1,0:T(8,128)(2,1)S(1)}, bf16[256,1536]{1,0:T(8,128)(2,1)S(1)}, u32[]{:S(2)}, u32[]{:S(2)}) collective-permute-start(bf16[256,1536]{1,0:T(8,128)(2,1)S(1)} %collective-permute-done.10), channel_id=1, source_target_pairs={{0,1},{1,2},{2,3},{3,0},{4,5},{5,6},{6,7},{7,4},{8,11},{9,8},{10,9... | collective-permute-start | bytes 2359304 | tf_op jit(solution)/shard_map/ppermute | solution.py:29
  72.0 3.0 %collective-permute-start.6 = (bf16[224,2048]{1,0:T(8,128)(2,1)S(1)}, bf16[224,2048]{1,0:T(8,128)(2,1)S(1)}, u32[]{:S(2)}, u32[]{:S(2)}) collective-permute-start(bf16[224,2048]{1,0:T(8,128)(2,1)S(1)} %fusion.10), channel_id=1, source_target_pairs={{0,4},{1,5},{2,6},{3,7},{4,0},{5,1},{6,2},{7,3},{8,12},{9,13},{10,... | collective-permute-start | bytes 2752520 | tf_op jit(solution)/shard_map/ppermute | solution.py:20
  75.4 0.4 fusion.28
  75.8 4.8 %collective-permute-done.11 = bf16[256,1536]{1,0:T(8,128)(2,1)S(1)} collective-permute-done((bf16[256,1536]{1,0:T(8,128)(2,1)S(1)}, bf16[256,1536]{1,0:T(8,128)(2,1)S(1)}, u32[]{:S(2)}, u32[]{:S(2)}) %collective-permute-start.11) | collective-permute-done | bytes 786464 | tf_op jit(solution)/shard_map/ppermute | solution.py:29
  81.0 0.4 fusion.11
  81.4 2.8 %collective-permute-start.14 = (bf16[224,1536]{1,0:T(8,128)(2,1)S(1)}, bf16[224,1536]{1,0:T(8,128)(2,1)S(1)}, u32[]{:S(2)}, u32[]{:S(2)}) collective-permute-start(bf16[224,1536]{1,0:T(8,128)(2,1)S(1)} %fusion.11), channel_id=1, source_target_pairs={{0,4},{1,5},{2,6},{3,7},{4,0},{5,1},{6,2},{7,3},{8,12},{9,13},{10,... | collective-permute-start | bytes 2064392 | tf_op jit(solution)/shard_map/ppermute | solution.py:20
  84.2 16.3 %collective-permute-done.6 = bf16[224,2048]{1,0:T(8,128)(2,1)S(1)} collective-permute-done((bf16[224,2048]{1,0:T(8,128)(2,1)S(1)}, bf16[224,2048]{1,0:T(8,128)(2,1)S(1)}, u32[]{:S(2)}, u32[]{:S(2)}) %collective-permute-start.6) | collective-permute-done | bytes 917536 | tf_op jit(solution)/shard_map/ppermute | solution.py:20
  100.5 0.8 fusion.23
  101.3 0.7 collective-permute-start.13
  102.7 22.4 %collective-permute-done.14 = bf16[224,1536]{1,0:T(8,128)(2,1)S(1)} collective-permute-done((bf16[224,1536]{1,0:T(8,128)(2,1)S(1)}, bf16[224,1536]{1,0:T(8,128)(2,1)S(1)}, u32[]{:S(2)}, u32[]{:S(2)}) %collective-permute-start.14) | collective-permute-done | bytes 688160 | tf_op jit(solution)/shard_map/ppermute | solution.py:20
  125.1 0.6 fusion.24
  125.7 0.6 collective-permute-start.18
  126.3 0.4 fusion.22
  126.8 3.5 %collective-permute-start.16 = (bf16[224,2048]{1,0:T(8,128)(2,1)S(1)}, bf16[224,2048]{1,0:T(8,128)(2,1)S(1)}, u32[]{:S(2)}, u32[]{:S(2)}) collective-permute-start(bf16[224,2048]{1,0:T(8,128)(2,1)S(1)} %fusion.22), channel_id=1, source_target_pairs={{0,240},{8,248},{16,0},{24,8},{32,16},{40,24},{48,32},{56,40},{64,... | collective-permute-start | bytes 2752520 | tf_op jit(solution)/shard_map/ppermute | solution.py:16
  130.2 3.0 %add_multiply_fusion = f32[224,3584]{1,0:T(8,128)S(1)} fusion(bf16[224,3584]{1,0:T(8,128)(2,1)S(1)} %collective-permute-done.8, bf16[224,3584]{1,0:T(8,128)(2,1)S(1)} %collective-permute-done.7, bf16[224,3584]{1,0:T(8,128)(2,1)} %collective-permute-done.1, bf16[224,3584]{1,0:T(8,128)(2,1)} %collective-permute-done, f32[1,224,3584]{2,1,0:T(8,128)S(1)} %copy-done), kind=kLoop, calls=%fused_computation.4 | loop fusion | flops 8028160 | bytes 12845056 | tf_op jit(solution)/shard_map/div | solution.py:37
  133.8 9.6 %collective-permute-done.18 = bf16[224,1536]{1,0:T(8,128)(2,1)S(1)} collective-permute-done((bf16[224,1536]{1,0:T(8,128)(2,1)S(1)}, bf16[224,1536]{1,0:T(8,128)(2,1)S(1)}, u32[]{:S(2)}, u32[]{:S(2)}) %collective-permute-start.18) | collective-permute-done | bytes 688160 | tf_op jit(solution)/shard_map/ppermute | solution.py:16
  143.8 6.1 %collective-permute-start.20 = (bf16[224,1536]{1,0:T(8,128)(2,1)S(1)}, bf16[224,1536]{1,0:T(8,128)(2,1)S(1)}, u32[]{:S(2)}, u32[]{:S(2)}) collective-permute-start(bf16[224,1536]{1,0:T(8,128)(2,1)S(1)} %fusion.21), channel_id=1, source_target_pairs={{0,240},{8,248},{16,0},{24,8},{32,16},{40,24},{48,32},{56,40},{64,... | collective-permute-start | bytes 2064392 | tf_op jit(solution)/shard_map/ppermute | solution.py:16
  149.9 0.5 collective-permute-done.16
  150.4 8.8 %collective-permute-done.15 = bf16[224,2048]{1,0:T(8,128)(2,1)S(1)} collective-permute-done((bf16[224,2048]{1,0:T(8,128)(2,1)S(1)}, bf16[224,2048]{1,0:T(8,128)(2,1)S(1)}, u32[]{:S(2)}, u32[]{:S(2)}) %collective-permute-start.15) | collective-permute-done | bytes 917536 | tf_op jit(solution)/shard_map/ppermute | solution.py:16
  159.2 0.8 multiply_convert_fusion
  159.9 0.8 fusion.13
  160.7 4.5 %collective-permute-done.20 = bf16[224,1536]{1,0:T(8,128)(2,1)S(1)} collective-permute-done((bf16[224,1536]{1,0:T(8,128)(2,1)S(1)}, bf16[224,1536]{1,0:T(8,128)(2,1)S(1)}, u32[]{:S(2)}, u32[]{:S(2)}) %collective-permute-start.20) | collective-permute-done | bytes 688160 | tf_op jit(solution)/shard_map/ppermute | solution.py:16
  165.2 7.2 %collective-permute-done.19 = bf16[224,1536]{1,0:T(8,128)(2,1)S(1)} collective-permute-done((bf16[224,1536]{1,0:T(8,128)(2,1)S(1)}, bf16[224,1536]{1,0:T(8,128)(2,1)S(1)}, u32[]{:S(2)}, u32[]{:S(2)}) %collective-permute-start.19) | collective-permute-done | bytes 688160 | tf_op jit(solution)/shard_map/ppermute | solution.py:16
  172.4 0.5 multiply_convert_fusion.1
  172.9 1.3 maximum_bitcast_fusion
  174.2 0.6 fusion.15
  174.9 1.7 copy-done.2
  (36 shorter events, 3.6 us)
Async XLA Ops:
  3.9 5.3 %copy-start.1 = (bf16[1,256,3584]{2,1,0:T(8,128)(2,1)S(1)}, bf16[1,256,3584]{2,1,0:T(8,128)(2,1)}, u32[]{:S(2)}) copy-start(bf16[1,256,3584]{2,1,0:T(8,128)(2,1)} %param.5) | copy-start | bytes 5505028
  3.9 24.4 %collective-permute-start = (bf16[224,3584]{1,0:T(8,128)(2,1)}, bf16[224,3584]{1,0:T(8,128)(2,1)}, u32[]{:S(2)}, u32[]{:S(2)}) collective-permute-start(bf16[224,3584]{1,0:T(8,128)(2,1)} %bitcast_convert_fusion), channel_id=1, source_target_pairs={{0,8},{8,16},{16,24},{24,32},{32,40},{40,48},{48,56},{56,64},{64,7... | collective-permute-start | bytes 4816904 | tf_op jit(solution)/shard_map/ppermute | solution.py:16
  6.9 21.4 %collective-permute-start.1 = (bf16[224,3584]{1,0:T(8,128)(2,1)}, bf16[224,3584]{1,0:T(8,128)(2,1)}, u32[]{:S(2)}, u32[]{:S(2)}) collective-permute-start(bf16[224,3584]{1,0:T(8,128)(2,1)} %bitcast_convert_fusion), channel_id=1, source_target_pairs={{0,248},{8,0},{16,8},{24,16},{32,24},{40,32},{48,40},{56,48},{64,5... | collective-permute-start | bytes 4816904 | tf_op jit(solution)/shard_map/ppermute | solution.py:16
  10.2 14.6 %collective-permute-start.2 = (bf16[256,2048]{1,0:T(8,128)(2,1)}, bf16[256,2048]{1,0:T(8,128)(2,1)}, u32[]{:S(2)}, u32[]{:S(2)}) collective-permute-start(bf16[256,2048]{1,0:T(8,128)(2,1)} %slice.51), channel_id=1, source_target_pairs={{0,1},{1,2},{2,3},{3,0},{4,5},{5,6},{6,7},{7,4},{8,11},{9,8},{10,9... | collective-permute-start | bytes 3145736 | tf_op jit(solution)/shard_map/ppermute | solution.py:29
  12.8 28.4 %collective-permute-start.3 = (bf16[224,1024]{1,0:T(8,128)(2,1)}, bf16[224,1024]{1,0:T(8,128)(2,1)S(1)}, u32[]{:S(2)}, u32[]{:S(2)}) collective-permute-start(bf16[224,1024]{1,0:T(8,128)(2,1)} %get-tuple-element.41), channel_id=1, source_target_pairs={{0,4},{1,5},{2,6},{3,7},{4,0},{5,1},{6,2},{7,3},{8,12},{9,13},{10,... | collective-permute-start | bytes 1376264 | tf_op jit(solution)/shard_map/ppermute | solution.py:20
  15.6 12.6 %copy-start = (f32[1,224,3584]{2,1,0:T(8,128)S(1)}, f32[1,224,3584]{2,1,0:T(8,128)}, u32[]{:S(2)}) copy-start(f32[1,224,3584]{2,1,0:T(8,128)} %param.6) | copy-start | bytes 9633796
  24.8 20.3 %collective-permute-start.4 = (bf16[256,2048]{1,0:T(8,128)(2,1)}, bf16[256,2048]{1,0:T(8,128)(2,1)S(1)}, u32[]{:S(2)}, u32[]{:S(2)}) collective-permute-start(bf16[256,2048]{1,0:T(8,128)(2,1)} %collective-permute-done.2), channel_id=1, source_target_pairs={{0,1},{1,2},{2,3},{3,0},{4,5},{5,6},{6,7},{7,4},{8,11},{9,8},{10,9... | collective-permute-start | bytes 3145736 | tf_op jit(solution)/shard_map/ppermute | solution.py:29
  28.2 23.1 %collective-permute-start.9 = (bf16[256,1536]{1,0:T(8,128)(2,1)S(1)}, bf16[256,1536]{1,0:T(8,128)(2,1)S(1)}, u32[]{:S(2)}, u32[]{:S(2)}) collective-permute-start(bf16[256,1536]{1,0:T(8,128)(2,1)S(1)} %slice.50), channel_id=1, source_target_pairs={{0,1},{1,2},{2,3},{3,0},{4,5},{5,6},{6,7},{7,4},{8,11},{9,8},{10,9... | collective-permute-start | bytes 2359304 | tf_op jit(solution)/shard_map/ppermute | solution.py:29
  41.1 43.1 %collective-permute-start.7 = (bf16[224,3584]{1,0:T(8,128)(2,1)S(1)}, bf16[224,3584]{1,0:T(8,128)(2,1)S(1)}, u32[]{:S(2)}, u32[]{:S(2)}) collective-permute-start(bf16[224,3584]{1,0:T(8,128)(2,1)S(1)} %fusion.16), channel_id=1, source_target_pairs={{0,16},{8,24},{16,32},{24,40},{32,48},{40,56},{48,64},{56,72},{64,... | collective-permute-start | bytes 4816904 | tf_op jit(solution)/shard_map/ppermute | solution.py:16
  41.1 43.1 %collective-permute-start.8 = (bf16[224,3584]{1,0:T(8,128)(2,1)S(1)}, bf16[224,3584]{1,0:T(8,128)(2,1)S(1)}, u32[]{:S(2)}, u32[]{:S(2)}) collective-permute-start(bf16[224,3584]{1,0:T(8,128)(2,1)S(1)} %fusion.16), channel_id=1, source_target_pairs={{0,240},{8,248},{16,0},{24,8},{32,16},{40,24},{48,32},{56,40},{64,... | collective-permute-start | bytes 4816904 | tf_op jit(solution)/shard_map/ppermute | solution.py:16
  45.1 14.7 %collective-permute-start.5 = (bf16[256,2048]{1,0:T(8,128)(2,1)S(1)}, bf16[256,2048]{1,0:T(8,128)(2,1)S(1)}, u32[]{:S(2)}, u32[]{:S(2)}) collective-permute-start(bf16[256,2048]{1,0:T(8,128)(2,1)S(1)} %collective-permute-done.4), channel_id=1, source_target_pairs={{0,1},{1,2},{2,3},{3,0},{4,5},{5,6},{6,7},{7,4},{8,11},{9,8},{10,9... | collective-permute-start | bytes 3145736 | tf_op jit(solution)/shard_map/ppermute | solution.py:29
  51.3 16.9 %collective-permute-start.10 = (bf16[256,1536]{1,0:T(8,128)(2,1)S(1)}, bf16[256,1536]{1,0:T(8,128)(2,1)S(1)}, u32[]{:S(2)}, u32[]{:S(2)}) collective-permute-start(bf16[256,1536]{1,0:T(8,128)(2,1)S(1)} %collective-permute-done.9), channel_id=1, source_target_pairs={{0,1},{1,2},{2,3},{3,0},{4,5},{5,6},{6,7},{7,4},{8,11},{9,8},{10,9... | collective-permute-start | bytes 2359304 | tf_op jit(solution)/shard_map/ppermute | solution.py:29
  68.3 12.3 %collective-permute-start.11 = (bf16[256,1536]{1,0:T(8,128)(2,1)S(1)}, bf16[256,1536]{1,0:T(8,128)(2,1)S(1)}, u32[]{:S(2)}, u32[]{:S(2)}) collective-permute-start(bf16[256,1536]{1,0:T(8,128)(2,1)S(1)} %collective-permute-done.10), channel_id=1, source_target_pairs={{0,1},{1,2},{2,3},{3,0},{4,5},{5,6},{6,7},{7,4},{8,11},{9,8},{10,9... | collective-permute-start | bytes 2359304 | tf_op jit(solution)/shard_map/ppermute | solution.py:29
  72.0 28.4 %collective-permute-start.6 = (bf16[224,2048]{1,0:T(8,128)(2,1)S(1)}, bf16[224,2048]{1,0:T(8,128)(2,1)S(1)}, u32[]{:S(2)}, u32[]{:S(2)}) collective-permute-start(bf16[224,2048]{1,0:T(8,128)(2,1)S(1)} %fusion.10), channel_id=1, source_target_pairs={{0,4},{1,5},{2,6},{3,7},{4,0},{5,1},{6,2},{7,3},{8,12},{9,13},{10,... | collective-permute-start | bytes 2752520 | tf_op jit(solution)/shard_map/ppermute | solution.py:20
  81.0 19.5 %copy-start.3 = (bf16[1,224,3584]{2,1,0:T(8,128)(2,1)S(1)}, bf16[1,224,3584]{2,1,0:T(8,128)(2,1)}, u32[]{:S(2)}) copy-start(bf16[1,224,3584]{2,1,0:T(8,128)(2,1)} %param.7) | copy-start | bytes 4816900
  81.4 43.7 %collective-permute-start.14 = (bf16[224,1536]{1,0:T(8,128)(2,1)S(1)}, bf16[224,1536]{1,0:T(8,128)(2,1)S(1)}, u32[]{:S(2)}, u32[]{:S(2)}) collective-permute-start(bf16[224,1536]{1,0:T(8,128)(2,1)S(1)} %fusion.11), channel_id=1, source_target_pairs={{0,4},{1,5},{2,6},{3,7},{4,0},{5,1},{6,2},{7,3},{8,12},{9,13},{10,... | collective-permute-start | bytes 2064392 | tf_op jit(solution)/shard_map/ppermute | solution.py:20
  101.2 25.1 %collective-permute-start.12 = (bf16[224,2048]{1,0:T(8,128)(2,1)S(1)}, bf16[224,2048]{1,0:T(8,128)(2,1)S(1)}, u32[]{:S(2)}, u32[]{:S(2)}) collective-permute-start(bf16[224,2048]{1,0:T(8,128)(2,1)S(1)} %get-tuple-element.50), channel_id=1, source_target_pairs={{0,8},{8,16},{16,24},{24,32},{32,40},{40,48},{48,56},{56,64},{64,7... | collective-permute-start | bytes 2752520 | tf_op jit(solution)/shard_map/ppermute | solution.py:16
  101.3 25.0 %collective-permute-start.13 = (bf16[224,2048]{1,0:T(8,128)(2,1)S(1)}, bf16[224,2048]{1,0:T(8,128)(2,1)S(1)}, u32[]{:S(2)}, u32[]{:S(2)}) collective-permute-start(bf16[224,2048]{1,0:T(8,128)(2,1)S(1)} %get-tuple-element.50), channel_id=1, source_target_pairs={{0,248},{8,0},{16,8},{24,16},{32,24},{40,32},{48,40},{56,48},{64,5... | collective-permute-start | bytes 2752520 | tf_op jit(solution)/shard_map/ppermute | solution.py:16
  125.7 8.2 %collective-permute-start.17 = (bf16[224,1536]{1,0:T(8,128)(2,1)S(1)}, bf16[224,1536]{1,0:T(8,128)(2,1)S(1)}, u32[]{:S(2)}, u32[]{:S(2)}) collective-permute-start(bf16[224,1536]{1,0:T(8,128)(2,1)S(1)} %get-tuple-element.35), channel_id=1, source_target_pairs={{0,8},{8,16},{16,24},{24,32},{32,40},{40,48},{48,56},{56,64},{64,7... | collective-permute-start | bytes 2064392 | tf_op jit(solution)/shard_map/ppermute | solution.py:16
  125.7 17.7 %collective-permute-start.18 = (bf16[224,1536]{1,0:T(8,128)(2,1)S(1)}, bf16[224,1536]{1,0:T(8,128)(2,1)S(1)}, u32[]{:S(2)}, u32[]{:S(2)}) collective-permute-start(bf16[224,1536]{1,0:T(8,128)(2,1)S(1)} %get-tuple-element.35), channel_id=1, source_target_pairs={{0,248},{8,0},{16,8},{24,16},{32,24},{40,32},{48,40},{56,48},{64,5... | collective-permute-start | bytes 2064392 | tf_op jit(solution)/shard_map/ppermute | solution.py:16
  126.8 23.6 %collective-permute-start.16 = (bf16[224,2048]{1,0:T(8,128)(2,1)S(1)}, bf16[224,2048]{1,0:T(8,128)(2,1)S(1)}, u32[]{:S(2)}, u32[]{:S(2)}) collective-permute-start(bf16[224,2048]{1,0:T(8,128)(2,1)S(1)} %fusion.22), channel_id=1, source_target_pairs={{0,240},{8,248},{16,0},{24,8},{32,16},{40,24},{48,32},{56,40},{64,... | collective-permute-start | bytes 2752520 | tf_op jit(solution)/shard_map/ppermute | solution.py:16
  130.2 28.9 %collective-permute-start.15 = (bf16[224,2048]{1,0:T(8,128)(2,1)S(1)}, bf16[224,2048]{1,0:T(8,128)(2,1)S(1)}, u32[]{:S(2)}, u32[]{:S(2)}) collective-permute-start(bf16[224,2048]{1,0:T(8,128)(2,1)S(1)} %fusion.22), channel_id=1, source_target_pairs={{0,16},{8,24},{16,32},{24,40},{32,48},{40,56},{48,64},{56,72},{64,... | collective-permute-start | bytes 2752520 | tf_op jit(solution)/shard_map/ppermute | solution.py:16
  143.8 21.4 %collective-permute-start.20 = (bf16[224,1536]{1,0:T(8,128)(2,1)S(1)}, bf16[224,1536]{1,0:T(8,128)(2,1)S(1)}, u32[]{:S(2)}, u32[]{:S(2)}) collective-permute-start(bf16[224,1536]{1,0:T(8,128)(2,1)S(1)} %fusion.21), channel_id=1, source_target_pairs={{0,240},{8,248},{16,0},{24,8},{32,16},{40,24},{48,32},{56,40},{64,... | collective-permute-start | bytes 2064392 | tf_op jit(solution)/shard_map/ppermute | solution.py:16
  149.9 22.5 %collective-permute-start.19 = (bf16[224,1536]{1,0:T(8,128)(2,1)S(1)}, bf16[224,1536]{1,0:T(8,128)(2,1)S(1)}, u32[]{:S(2)}, u32[]{:S(2)}) collective-permute-start(bf16[224,1536]{1,0:T(8,128)(2,1)S(1)} %fusion.21), channel_id=1, source_target_pairs={{0,16},{8,24},{16,32},{24,40},{32,48},{40,56},{48,64},{56,72},{64,... | collective-permute-start | bytes 2064392 | tf_op jit(solution)/shard_map/ppermute | solution.py:16
  174.9 1.7 copy-start.2

commit v4 on v3

--- a/solution.py
+++ b/solution.py
@@ -116,13 +116,14 @@
     v1b16 = v1_b.astype(bf16)
     vb2_low, vb2_up = passed_along(v1b16, 2), passed_along(v1b16, -2)
 
+    momentum_a = third(v1_a, va2_low, va2_up)
+    momentum_b = third(v1_b, vb2_low, vb2_up)
     out_p = p_mixed
-    out_m = jnp.zeros(mom.shape, bf16)
-    for (lo, hi), v1, low, up in ((CUTS[0], v1_a, va2_low, va2_up), (CUTS[1], v1_b, vb2_low, vb2_up)):
-        velocity = third(v1, low, up)
-        weights = p_mixed[:, lo:hi] - learn_rate * velocity
-        out_p = lax.dynamic_update_slice(out_p, weights, (0, lo))
-        out_m = lax.dynamic_update_slice(out_m, velocity.astype(bf16), (0, lo))
+    for (lo, hi), velocity in ((CUTS[0], momentum_a), (CUTS[1], momentum_b)):
+        out_p = lax.dynamic_update_slice(out_p, p_mixed[:, lo:hi] - learn_rate * velocity, (0, lo))
+    out_p, vb2_low, vb2_up = tied(out_p, vb2_low, vb2_up)
+    last = third(v1_b, vb2_low, vb2_up)
+    out_m = jnp.concatenate([momentum_a.astype(bf16), last.astype(bf16)], 1)
     return (out_p[None], out_m[None])
 
 

time: 177 us -> 176 us (level)
  transfers between devices with their start and end apart: 21 -> 21, of which waited for: 13 -> 12; matrix products, arithmetic and copies ran while one was open for 12% -> 11% of each run, Pallas kernels for 0% -> 0%
where the time goes in v4:
time: 176 us
  waiting for transfers between devices  107 us (61%)
  starting transfers between devices  39.3 us (22%)
  other arithmetic  15.4 us (9%)
  matrix products  9.15 us (5%)
  local copies, waits for them, and re-layouts  4.05 us (2%)
    ppermute x3, waiting for transfers between devices, swapped(): return lax.ppermute(value, 'tensor', [(t, t ^ 4) for t in range(8)])  48.9 us
    ppermute x12, waiting for transfers between devices, passed_along(): return lax.ppermute(value, 'replica', pairs)  29.6 us
    ppermute x6, waiting for transfers between devices, ring_step(): return lax.ppermute(value, BOTH, pairs)  28.6 us
    ppermute x12, starting transfers between devices, passed_along(): return lax.ppermute(value, 'replica', pairs)  17.8 us
    ppermute x6, starting transfers between devices, ring_step(): return lax.ppermute(value, BOTH, pairs)  12.9 us
    ppermute x3, starting transfers between devices, swapped(): return lax.ppermute(value, 'tensor', [(t, t ^ 4) for t in range(8)])  8.59 us
    dot_general x8, matrix products, gradient(): a = jnp.dot(own_by_step[step], blocks[step], preferred_element_type=f32)  4.85 us
    dot_general x8, matrix products, gradient(): b = jnp.dot(oth_by_step[step], blocks[step], preferred_element_type=f32)  4.3 us
  transfers between devices with their start and end apart: 21, of which 12 were waited for; matrix products, arithmetic and copies ran while one was open for 11% of the time, Pallas kernels for 0%

profile of v4, /device:TPU:1, one launch (start us, length us, event | category | flops | bytes accessed | tf_op | source)
XLA Modules:
  0.0 175.9 jit_solution(11128157982674615089)
XLA Ops:
  0.6 3.2 %bitcast_convert_fusion = bf16[224,3584]{1,0:T(8,128)(2,1)} fusion(f32[1,224,3584]{2,1,0:T(8,128)} %param.6), kind=kLoop, calls=%fused_computation.1 | loop fusion | flops 802816 | bytes 4816896 | tf_op jit(solution)/shard_map/convert_element_type | solution.py:49
  3.9 3.0 %collective-permute-start = (bf16[224,3584]{1,0:T(8,128)(2,1)}, bf16[224,3584]{1,0:T(8,128)(2,1)}, u32[]{:S(2)}, u32[]{:S(2)}) collective-permute-start(bf16[224,3584]{1,0:T(8,128)(2,1)} %bitcast_convert_fusion), channel_id=1, source_target_pairs={{0,8},{8,16},{16,24},{24,32},{32,40},{40,48},{48,56},{56,64},{64,7... | collective-permute-start | bytes 4816904 | tf_op jit(solution)/shard_map/ppermute | solution.py:16
  7.1 2.0 %broadcast_select_fusion = (bf16[224,1024]{1,0:T(8,128)(2,1)S(1)}, bf16[224,1024]{1,0:T(8,128)(2,1)}) fusion(pred[]{:T(512)S(6)} %eq.35, bf16[224,2048]{1,0:T(8,128)(2,1)} %bitcast.56), kind=kLoop, calls=%fused_computation.34 | loop fusion | flops 458752 | bytes 1835009 | tf_op jit(solution)/shard_map/jit(_where)/select_n | solution.py:55
  9.1 1.1 slice.51
  10.2 2.5 %collective-permute-start.2 = (bf16[256,2048]{1,0:T(8,128)(2,1)}, bf16[256,2048]{1,0:T(8,128)(2,1)}, u32[]{:S(2)}, u32[]{:S(2)}) collective-permute-start(bf16[256,2048]{1,0:T(8,128)(2,1)} %slice.51), channel_id=1, source_target_pairs={{0,1},{1,2},{2,3},{3,0},{4,5},{5,6},{6,7},{7,4},{8,11},{9,8},{10,9... | collective-permute-start | bytes 3145736 | tf_op jit(solution)/shard_map/ppermute | solution.py:29
  12.7 2.7 %collective-permute-start.3 = (bf16[224,1024]{1,0:T(8,128)(2,1)}, bf16[224,1024]{1,0:T(8,128)(2,1)S(1)}, u32[]{:S(2)}, u32[]{:S(2)}) collective-permute-start(bf16[224,1024]{1,0:T(8,128)(2,1)} %get-tuple-element.49), channel_id=1, source_target_pairs={{0,4},{1,5},{2,6},{3,7},{4,0},{5,1},{6,2},{7,3},{8,12},{9,13},{10,... | collective-permute-start | bytes 1376264 | tf_op jit(solution)/shard_map/ppermute | solution.py:20
  15.7 0.4 fusion.15
  16.1 8.7 %collective-permute-done.2 = bf16[256,2048]{1,0:T(8,128)(2,1)} collective-permute-done((bf16[256,2048]{1,0:T(8,128)(2,1)}, bf16[256,2048]{1,0:T(8,128)(2,1)}, u32[]{:S(2)}, u32[]{:S(2)}) %collective-permute-start.2) | collective-permute-done | bytes 1048608 | tf_op jit(solution)/shard_map/ppermute | solution.py:29
  24.8 3.4 %collective-permute-start.4 = (bf16[256,2048]{1,0:T(8,128)(2,1)}, bf16[256,2048]{1,0:T(8,128)(2,1)S(1)}, u32[]{:S(2)}, u32[]{:S(2)}) collective-permute-start(bf16[256,2048]{1,0:T(8,128)(2,1)} %collective-permute-done.2), channel_id=1, source_target_pairs={{0,1},{1,2},{2,3},{3,0},{4,5},{5,6},{6,7},{7,4},{8,11},{9,8},{10,9... | collective-permute-start | bytes 3145736 | tf_op jit(solution)/shard_map/ppermute | solution.py:29
  28.3 2.6 %fusion.14 = bf16[224,3584]{1,0:T(8,128)(2,1)S(1)} fusion(bf16[224,3584]{1,0:T(8,128)(2,1)} %collective-permute-done.1, bf16[224,3584]{1,0:T(8,128)(2,1)} %collective-permute-done, f32[1,224,3584]{2,1,0:T(8,128)S(1)} %copy-done), kind=kLoop, calls=%fused_computation.33 | loop fusion | flops 4816896 | bytes 8028160 | tf_op jit(solution)/shard_map/convert_element_type | solution.py:68
  30.8 10.3 %collective-permute-done.3 = bf16[224,1024]{1,0:T(8,128)(2,1)S(1)} collective-permute-done((bf16[224,1024]{1,0:T(8,128)(2,1)}, bf16[224,1024]{1,0:T(8,128)(2,1)S(1)}, u32[]{:S(2)}, u32[]{:S(2)}) %collective-permute-start.3) | collective-permute-done | bytes 458784 | tf_op jit(solution)/shard_map/ppermute | solution.py:20
  41.1 3.6 %collective-permute-start.8 = (bf16[224,3584]{1,0:T(8,128)(2,1)S(1)}, bf16[224,3584]{1,0:T(8,128)(2,1)S(1)}, u32[]{:S(2)}, u32[]{:S(2)}) collective-permute-start(bf16[224,3584]{1,0:T(8,128)(2,1)S(1)} %fusion.14), channel_id=1, source_target_pairs={{0,240},{8,248},{16,0},{24,8},{32,16},{40,24},{48,32},{56,40},{64,... | collective-permute-start | bytes 4816904 | tf_op jit(solution)/shard_map/ppermute | solution.py:16
  44.7 0.4 fusion.17
  45.1 2.8 %collective-permute-start.5 = (bf16[256,2048]{1,0:T(8,128)(2,1)S(1)}, bf16[256,2048]{1,0:T(8,128)(2,1)S(1)}, u32[]{:S(2)}, u32[]{:S(2)}) collective-permute-start(bf16[256,2048]{1,0:T(8,128)(2,1)S(1)} %collective-permute-done.4), channel_id=1, source_target_pairs={{0,1},{1,2},{2,3},{3,0},{4,5},{5,6},{6,7},{7,4},{8,11},{9,8},{10,9... | collective-permute-start | bytes 3145736 | tf_op jit(solution)/shard_map/ppermute | solution.py:29
  48.0 1.7 convolution_add_fusion.7
  49.6 1.7 convolution_add_fusion.5
  51.3 0.7 collective-permute-start.10
  52.4 7.5 %collective-permute-done.5 = bf16[256,2048]{1,0:T(8,128)(2,1)S(1)} collective-permute-done((bf16[256,2048]{1,0:T(8,128)(2,1)S(1)}, bf16[256,2048]{1,0:T(8,128)(2,1)S(1)}, u32[]{:S(2)}, u32[]{:S(2)}) %collective-permute-start.5) | collective-permute-done | bytes 1048608 | tf_op jit(solution)/shard_map/ppermute | solution.py:29
  59.8 0.4 fusion.23
  60.2 0.5 fusion.10
  60.7 7.6 %collective-permute-done.10 = bf16[256,1536]{1,0:T(8,128)(2,1)S(1)} collective-permute-done((bf16[256,1536]{1,0:T(8,128)(2,1)S(1)}, bf16[256,1536]{1,0:T(8,128)(2,1)S(1)}, u32[]{:S(2)}, u32[]{:S(2)}) %collective-permute-start.10) | collective-permute-done | bytes 786464 | tf_op jit(solution)/shard_map/ppermute | solution.py:29
  68.3 3.4 %collective-permute-start.11 = (bf16[256,1536]{1,0:T(8,128)(2,1)S(1)}, bf16[256,1536]{1,0:T(8,128)(2,1)S(1)}, u32[]{:S(2)}, u32[]{:S(2)}) collective-permute-start(bf16[256,1536]{1,0:T(8,128)(2,1)S(1)} %collective-permute-done.10), channel_id=1, source_target_pairs={{0,1},{1,2},{2,3},{3,0},{4,5},{5,6},{6,7},{7,4},{8,11},{9,8},{10,9... | collective-permute-start | bytes 2359304 | tf_op jit(solution)/shard_map/ppermute | solution.py:29
  72.0 3.0 %collective-permute-start.6 = (bf16[224,2048]{1,0:T(8,128)(2,1)S(1)}, bf16[224,2048]{1,0:T(8,128)(2,1)S(1)}, u32[]{:S(2)}, u32[]{:S(2)}) collective-permute-start(bf16[224,2048]{1,0:T(8,128)(2,1)S(1)} %fusion.10), channel_id=1, source_target_pairs={{0,4},{1,5},{2,6},{3,7},{4,0},{5,1},{6,2},{7,3},{8,12},{9,13},{10,... | collective-permute-start | bytes 2752520 | tf_op jit(solution)/shard_map/ppermute | solution.py:20
  75.4 0.4 fusion.26
  75.8 4.8 %collective-permute-done.11 = bf16[256,1536]{1,0:T(8,128)(2,1)S(1)} collective-permute-done((bf16[256,1536]{1,0:T(8,128)(2,1)S(1)}, bf16[256,1536]{1,0:T(8,128)(2,1)S(1)}, u32[]{:S(2)}, u32[]{:S(2)}) %collective-permute-start.11) | collective-permute-done | bytes 786464 | tf_op jit(solution)/shard_map/ppermute | solution.py:29
  81.0 0.4 fusion.11
  81.3 2.8 %collective-permute-start.14 = (bf16[224,1536]{1,0:T(8,128)(2,1)S(1)}, bf16[224,1536]{1,0:T(8,128)(2,1)S(1)}, u32[]{:S(2)}, u32[]{:S(2)}) collective-permute-start(bf16[224,1536]{1,0:T(8,128)(2,1)S(1)} %fusion.11), channel_id=1, source_target_pairs={{0,4},{1,5},{2,6},{3,7},{4,0},{5,1},{6,2},{7,3},{8,12},{9,13},{10,... | collective-permute-start | bytes 2064392 | tf_op jit(solution)/shard_map/ppermute | solution.py:20
  84.2 16.3 %collective-permute-done.6 = bf16[224,2048]{1,0:T(8,128)(2,1)S(1)} collective-permute-done((bf16[224,2048]{1,0:T(8,128)(2,1)S(1)}, bf16[224,2048]{1,0:T(8,128)(2,1)S(1)}, u32[]{:S(2)}, u32[]{:S(2)}) %collective-permute-start.6) | collective-permute-done | bytes 917536 | tf_op jit(solution)/shard_map/ppermute | solution.py:20
  100.5 0.8 fusion.21
  101.4 0.7 collective-permute-start.13
  102.7 22.3 %collective-permute-done.14 = bf16[224,1536]{1,0:T(8,128)(2,1)S(1)} collective-permute-done((bf16[224,1536]{1,0:T(8,128)(2,1)S(1)}, bf16[224,1536]{1,0:T(8,128)(2,1)S(1)}, u32[]{:S(2)}, u32[]{:S(2)}) %collective-permute-start.14) | collective-permute-done | bytes 688160 | tf_op jit(solution)/shard_map/ppermute | solution.py:20
  125.1 0.6 fusion.22
  125.7 0.6 collective-permute-start.18
  126.3 0.4 fusion.20
  126.7 3.5 %collective-permute-start.16 = (bf16[224,2048]{1,0:T(8,128)(2,1)S(1)}, bf16[224,2048]{1,0:T(8,128)(2,1)S(1)}, u32[]{:S(2)}, u32[]{:S(2)}) collective-permute-start(bf16[224,2048]{1,0:T(8,128)(2,1)S(1)} %fusion.20), channel_id=1, source_target_pairs={{0,240},{8,248},{16,0},{24,8},{32,16},{40,24},{48,32},{56,40},{64,... | collective-permute-start | bytes 2752520 | tf_op jit(solution)/shard_map/ppermute | solution.py:16
  130.2 3.0 %add_multiply_fusion = f32[224,3584]{1,0:T(8,128)S(1)} fusion(bf16[224,3584]{1,0:T(8,128)(2,1)S(1)} %collective-permute-done.8, bf16[224,3584]{1,0:T(8,128)(2,1)S(1)} %collective-permute-done.7, bf16[224,3584]{1,0:T(8,128)(2,1)} %collective-permute-done.1, bf16[224,3584]{1,0:T(8,128)(2,1)} %collective-permute-done, f32[1,224,3584]{2,1,0:T(8,128)S(1)} %copy-done), kind=kLoop, calls=%fused_computation.4 | loop fusion | flops 8028160 | bytes 12845056 | tf_op jit(solution)/shard_map/div | solution.py:37
  133.2 1.7 copy-done.1
  134.9 8.5 %collective-permute-done.18 = bf16[224,1536]{1,0:T(8,128)(2,1)S(1)} collective-permute-done((bf16[224,1536]{1,0:T(8,128)(2,1)S(1)}, bf16[224,1536]{1,0:T(8,128)(2,1)S(1)}, u32[]{:S(2)}, u32[]{:S(2)}) %collective-permute-start.18) | collective-permute-done | bytes 688160 | tf_op jit(solution)/shard_map/ppermute | solution.py:16
  143.7 6.1 %collective-permute-start.20 = (bf16[224,1536]{1,0:T(8,128)(2,1)S(1)}, bf16[224,1536]{1,0:T(8,128)(2,1)S(1)}, u32[]{:S(2)}, u32[]{:S(2)}) collective-permute-start(bf16[224,1536]{1,0:T(8,128)(2,1)S(1)} %fusion.19), channel_id=1, source_target_pairs={{0,240},{8,248},{16,0},{24,8},{32,16},{40,24},{48,32},{56,40},{64,... | collective-permute-start | bytes 2064392 | tf_op jit(solution)/shard_map/ppermute | solution.py:16
  149.9 0.5 collective-permute-done.16
  150.3 8.8 %collective-permute-done.15 = bf16[224,2048]{1,0:T(8,128)(2,1)S(1)} collective-permute-done((bf16[224,2048]{1,0:T(8,128)(2,1)S(1)}, bf16[224,2048]{1,0:T(8,128)(2,1)S(1)}, u32[]{:S(2)}, u32[]{:S(2)}) %collective-permute-start.15) | collective-permute-done | bytes 917536 | tf_op jit(solution)/shard_map/ppermute | solution.py:16
  159.1 1.5 multiply_convert_fusion
  160.6 4.6 %collective-permute-done.20 = bf16[224,1536]{1,0:T(8,128)(2,1)S(1)} collective-permute-done((bf16[224,1536]{1,0:T(8,128)(2,1)S(1)}, bf16[224,1536]{1,0:T(8,128)(2,1)S(1)}, u32[]{:S(2)}, u32[]{:S(2)}) %collective-permute-start.20) | collective-permute-done | bytes 688160 | tf_op jit(solution)/shard_map/ppermute | solution.py:16
  165.2 7.2 %collective-permute-done.19 = bf16[224,1536]{1,0:T(8,128)(2,1)S(1)} collective-permute-done((bf16[224,1536]{1,0:T(8,128)(2,1)S(1)}, bf16[224,1536]{1,0:T(8,128)(2,1)S(1)}, u32[]{:S(2)}, u32[]{:S(2)}) %collective-permute-start.19) | collective-permute-done | bytes 688160 | tf_op jit(solution)/shard_map/ppermute | solution.py:16
  172.4 0.6 fusion.13
  173.0 0.5 multiply_convert_fusion.1
  173.5 1.2 copy-done.3
  174.6 1.3 maximum_bitcast_fusion
  (40 shorter events, 3.0 us)
Async XLA Ops:
  3.9 5.3 %copy-start.5 = (bf16[1,256,3584]{2,1,0:T(8,128)(2,1)S(1)}, bf16[1,256,3584]{2,1,0:T(8,128)(2,1)}, u32[]{:S(2)}) copy-start(bf16[1,256,3584]{2,1,0:T(8,128)(2,1)} %param.5) | copy-start | bytes 5505028
  3.9 24.4 %collective-permute-start = (bf16[224,3584]{1,0:T(8,128)(2,1)}, bf16[224,3584]{1,0:T(8,128)(2,1)}, u32[]{:S(2)}, u32[]{:S(2)}) collective-permute-start(bf16[224,3584]{1,0:T(8,128)(2,1)} %bitcast_convert_fusion), channel_id=1, source_target_pairs={{0,8},{8,16},{16,24},{24,32},{32,40},{40,48},{48,56},{56,64},{64,7... | collective-permute-start | bytes 4816904 | tf_op jit(solution)/shard_map/ppermute | solution.py:16
  6.9 21.4 %collective-permute-start.1 = (bf16[224,3584]{1,0:T(8,128)(2,1)}, bf16[224,3584]{1,0:T(8,128)(2,1)}, u32[]{:S(2)}, u32[]{:S(2)}) collective-permute-start(bf16[224,3584]{1,0:T(8,128)(2,1)} %bitcast_convert_fusion), channel_id=1, source_target_pairs={{0,248},{8,0},{16,8},{24,16},{32,24},{40,32},{48,40},{56,48},{64,5... | collective-permute-start | bytes 4816904 | tf_op jit(solution)/shard_map/ppermute | solution.py:16
  10.2 14.6 %collective-permute-start.2 = (bf16[256,2048]{1,0:T(8,128)(2,1)}, bf16[256,2048]{1,0:T(8,128)(2,1)}, u32[]{:S(2)}, u32[]{:S(2)}) collective-permute-start(bf16[256,2048]{1,0:T(8,128)(2,1)} %slice.51), channel_id=1, source_target_pairs={{0,1},{1,2},{2,3},{3,0},{4,5},{5,6},{6,7},{7,4},{8,11},{9,8},{10,9... | collective-permute-start | bytes 3145736 | tf_op jit(solution)/shard_map/ppermute | solution.py:29
  12.7 28.4 %collective-permute-start.3 = (bf16[224,1024]{1,0:T(8,128)(2,1)}, bf16[224,1024]{1,0:T(8,128)(2,1)S(1)}, u32[]{:S(2)}, u32[]{:S(2)}) collective-permute-start(bf16[224,1024]{1,0:T(8,128)(2,1)} %get-tuple-element.49), channel_id=1, source_target_pairs={{0,4},{1,5},{2,6},{3,7},{4,0},{5,1},{6,2},{7,3},{8,12},{9,13},{10,... | collective-permute-start | bytes 1376264 | tf_op jit(solution)/shard_map/ppermute | solution.py:20
  15.6 12.6 %copy-start = (f32[1,224,3584]{2,1,0:T(8,128)S(1)}, f32[1,224,3584]{2,1,0:T(8,128)}, u32[]{:S(2)}) copy-start(f32[1,224,3584]{2,1,0:T(8,128)} %param.6) | copy-start | bytes 9633796
  24.8 20.3 %collective-permute-start.4 = (bf16[256,2048]{1,0:T(8,128)(2,1)}, bf16[256,2048]{1,0:T(8,128)(2,1)S(1)}, u32[]{:S(2)}, u32[]{:S(2)}) collective-permute-start(bf16[256,2048]{1,0:T(8,128)(2,1)} %collective-permute-done.2), channel_id=1, source_target_pairs={{0,1},{1,2},{2,3},{3,0},{4,5},{5,6},{6,7},{7,4},{8,11},{9,8},{10,9... | collective-permute-start | bytes 3145736 | tf_op jit(solution)/shard_map/ppermute | solution.py:29
  28.2 23.1 %collective-permute-start.9 = (bf16[256,1536]{1,0:T(8,128)(2,1)S(1)}, bf16[256,1536]{1,0:T(8,128)(2,1)S(1)}, u32[]{:S(2)}, u32[]{:S(2)}) collective-permute-start(bf16[256,1536]{1,0:T(8,128)(2,1)S(1)} %slice.50), channel_id=1, source_target_pairs={{0,1},{1,2},{2,3},{3,0},{4,5},{5,6},{6,7},{7,4},{8,11},{9,8},{10,9... | collective-permute-start | bytes 2359304 | tf_op jit(solution)/shard_map/ppermute | solution.py:29
  41.1 43.0 %collective-permute-start.7 = (bf16[224,3584]{1,0:T(8,128)(2,1)S(1)}, bf16[224,3584]{1,0:T(8,128)(2,1)S(1)}, u32[]{:S(2)}, u32[]{:S(2)}) collective-permute-start(bf16[224,3584]{1,0:T(8,128)(2,1)S(1)} %fusion.14), channel_id=1, source_target_pairs={{0,16},{8,24},{16,32},{24,40},{32,48},{40,56},{48,64},{56,72},{64,... | collective-permute-start | bytes 4816904 | tf_op jit(solution)/shard_map/ppermute | solution.py:16
  41.1 43.0 %collective-permute-start.8 = (bf16[224,3584]{1,0:T(8,128)(2,1)S(1)}, bf16[224,3584]{1,0:T(8,128)(2,1)S(1)}, u32[]{:S(2)}, u32[]{:S(2)}) collective-permute-start(bf16[224,3584]{1,0:T(8,128)(2,1)S(1)} %fusion.14), channel_id=1, source_target_pairs={{0,240},{8,248},{16,0},{24,8},{32,16},{40,24},{48,32},{56,40},{64,... | collective-permute-start | bytes 4816904 | tf_op jit(solution)/shard_map/ppermute | solution.py:16
  45.1 14.7 %collective-permute-start.5 = (bf16[256,2048]{1,0:T(8,128)(2,1)S(1)}, bf16[256,2048]{1,0:T(8,128)(2,1)S(1)}, u32[]{:S(2)}, u32[]{:S(2)}) collective-permute-start(bf16[256,2048]{1,0:T(8,128)(2,1)S(1)} %collective-permute-done.4), channel_id=1, source_target_pairs={{0,1},{1,2},{2,3},{3,0},{4,5},{5,6},{6,7},{7,4},{8,11},{9,8},{10,9... | collective-permute-start | bytes 3145736 | tf_op jit(solution)/shard_map/ppermute | solution.py:29
  51.3 16.9 %collective-permute-start.10 = (bf16[256,1536]{1,0:T(8,128)(2,1)S(1)}, bf16[256,1536]{1,0:T(8,128)(2,1)S(1)}, u32[]{:S(2)}, u32[]{:S(2)}) collective-permute-start(bf16[256,1536]{1,0:T(8,128)(2,1)S(1)} %collective-permute-done.9), channel_id=1, source_target_pairs={{0,1},{1,2},{2,3},{3,0},{4,5},{5,6},{6,7},{7,4},{8,11},{9,8},{10,9... | collective-permute-start | bytes 2359304 | tf_op jit(solution)/shard_map/ppermute | solution.py:29
  68.3 12.3 %collective-permute-start.11 = (bf16[256,1536]{1,0:T(8,128)(2,1)S(1)}, bf16[256,1536]{1,0:T(8,128)(2,1)S(1)}, u32[]{:S(2)}, u32[]{:S(2)}) collective-permute-start(bf16[256,1536]{1,0:T(8,128)(2,1)S(1)} %collective-permute-done.10), channel_id=1, source_target_pairs={{0,1},{1,2},{2,3},{3,0},{4,5},{5,6},{6,7},{7,4},{8,11},{9,8},{10,9... | collective-permute-start | bytes 2359304 | tf_op jit(solution)/shard_map/ppermute | solution.py:29
  72.0 28.4 %collective-permute-start.6 = (bf16[224,2048]{1,0:T(8,128)(2,1)S(1)}, bf16[224,2048]{1,0:T(8,128)(2,1)S(1)}, u32[]{:S(2)}, u32[]{:S(2)}) collective-permute-start(bf16[224,2048]{1,0:T(8,128)(2,1)S(1)} %fusion.10), channel_id=1, source_target_pairs={{0,4},{1,5},{2,6},{3,7},{4,0},{5,1},{6,2},{7,3},{8,12},{9,13},{10,... | collective-permute-start | bytes 2752520 | tf_op jit(solution)/shard_map/ppermute | solution.py:20
  81.0 19.5 %copy-start.6 = (bf16[1,224,3584]{2,1,0:T(8,128)(2,1)S(1)}, bf16[1,224,3584]{2,1,0:T(8,128)(2,1)}, u32[]{:S(2)}) copy-start(bf16[1,224,3584]{2,1,0:T(8,128)(2,1)} %param.7) | copy-start | bytes 4816900
  81.3 43.7 %collective-permute-start.14 = (bf16[224,1536]{1,0:T(8,128)(2,1)S(1)}, bf16[224,1536]{1,0:T(8,128)(2,1)S(1)}, u32[]{:S(2)}, u32[]{:S(2)}) collective-permute-start(bf16[224,1536]{1,0:T(8,128)(2,1)S(1)} %fusion.11), channel_id=1, source_target_pairs={{0,4},{1,5},{2,6},{3,7},{4,0},{5,1},{6,2},{7,3},{8,12},{9,13},{10,... | collective-permute-start | bytes 2064392 | tf_op jit(solution)/shard_map/ppermute | solution.py:20
  101.3 25.0 %collective-permute-start.12 = (bf16[224,2048]{1,0:T(8,128)(2,1)S(1)}, bf16[224,2048]{1,0:T(8,128)(2,1)S(1)}, u32[]{:S(2)}, u32[]{:S(2)}) collective-permute-start(bf16[224,2048]{1,0:T(8,128)(2,1)S(1)} %get-tuple-element.58), channel_id=1, source_target_pairs={{0,8},{8,16},{16,24},{24,32},{32,40},{40,48},{48,56},{56,64},{64,7... | collective-permute-start | bytes 2752520 | tf_op jit(solution)/shard_map/ppermute | solution.py:16
  101.4 24.9 %collective-permute-start.13 = (bf16[224,2048]{1,0:T(8,128)(2,1)S(1)}, bf16[224,2048]{1,0:T(8,128)(2,1)S(1)}, u32[]{:S(2)}, u32[]{:S(2)}) collective-permute-start(bf16[224,2048]{1,0:T(8,128)(2,1)S(1)} %get-tuple-element.58), channel_id=1, source_target_pairs={{0,248},{8,0},{16,8},{24,16},{32,24},{40,32},{48,40},{56,48},{64,5... | collective-permute-start | bytes 2752520 | tf_op jit(solution)/shard_map/ppermute | solution.py:16
  125.6 9.3 %collective-permute-start.17 = (bf16[224,1536]{1,0:T(8,128)(2,1)S(1)}, bf16[224,1536]{1,0:T(8,128)(2,1)S(1)}, u32[]{:S(2)}, u32[]{:S(2)}) collective-permute-start(bf16[224,1536]{1,0:T(8,128)(2,1)S(1)} %get-tuple-element.38), channel_id=1, source_target_pairs={{0,8},{8,16},{16,24},{24,32},{32,40},{40,48},{48,56},{56,64},{64,7... | collective-permute-start | bytes 2064392 | tf_op jit(solution)/shard_map/ppermute | solution.py:16
  125.7 17.7 %collective-permute-start.18 = (bf16[224,1536]{1,0:T(8,128)(2,1)S(1)}, bf16[224,1536]{1,0:T(8,128)(2,1)S(1)}, u32[]{:S(2)}, u32[]{:S(2)}) collective-permute-start(bf16[224,1536]{1,0:T(8,128)(2,1)S(1)} %get-tuple-element.38), channel_id=1, source_target_pairs={{0,248},{8,0},{16,8},{24,16},{32,24},{40,32},{48,40},{56,48},{64,5... | collective-permute-start | bytes 2064392 | tf_op jit(solution)/shard_map/ppermute | solution.py:16
  126.7 23.6 %collective-permute-start.16 = (bf16[224,2048]{1,0:T(8,128)(2,1)S(1)}, bf16[224,2048]{1,0:T(8,128)(2,1)S(1)}, u32[]{:S(2)}, u32[]{:S(2)}) collective-permute-start(bf16[224,2048]{1,0:T(8,128)(2,1)S(1)} %fusion.20), channel_id=1, source_target_pairs={{0,240},{8,248},{16,0},{24,8},{32,16},{40,24},{48,32},{56,40},{64,... | collective-permute-start | bytes 2752520 | tf_op jit(solution)/shard_map/ppermute | solution.py:16
  130.2 28.9 %collective-permute-start.15 = (bf16[224,2048]{1,0:T(8,128)(2,1)S(1)}, bf16[224,2048]{1,0:T(8,128)(2,1)S(1)}, u32[]{:S(2)}, u32[]{:S(2)}) collective-permute-start(bf16[224,2048]{1,0:T(8,128)(2,1)S(1)} %fusion.20), channel_id=1, source_target_pairs={{0,16},{8,24},{16,32},{24,40},{32,48},{40,56},{48,64},{56,72},{64,... | collective-permute-start | bytes 2752520 | tf_op jit(solution)/shard_map/ppermute | solution.py:16
  133.2 1.7 copy-start.1
  134.9 24.2 %copy-start.4 = (f32[224,3584]{1,0:T(8,128)S(1)}, f32[224,3584]{1,0:T(8,128)}, u32[]{:S(2)}) copy-start(f32[224,3584]{1,0:T(8,128)} %copy-done.1) | copy-start | bytes 9633796
  143.7 28.7 %copy-start.2 = (f32[224,3584]{1,0:T(8,128)S(1)}, f32[224,3584]{1,0:T(8,128)}, u32[]{:S(2)}) copy-start(f32[224,3584]{1,0:T(8,128)} %copy-done.1) | copy-start | bytes 9633796
  143.7 21.4 %collective-permute-start.20 = (bf16[224,1536]{1,0:T(8,128)(2,1)S(1)}, bf16[224,1536]{1,0:T(8,128)(2,1)S(1)}, u32[]{:S(2)}, u32[]{:S(2)}) collective-permute-start(bf16[224,1536]{1,0:T(8,128)(2,1)S(1)} %fusion.19), channel_id=1, source_target_pairs={{0,240},{8,248},{16,0},{24,8},{32,16},{40,24},{48,32},{56,40},{64,... | collective-permute-start | bytes 2064392 | tf_op jit(solution)/shard_map/ppermute | solution.py:16
  149.9 22.5 %collective-permute-start.19 = (bf16[224,1536]{1,0:T(8,128)(2,1)S(1)}, bf16[224,1536]{1,0:T(8,128)(2,1)S(1)}, u32[]{:S(2)}, u32[]{:S(2)}) collective-permute-start(bf16[224,1536]{1,0:T(8,128)(2,1)S(1)} %fusion.19), channel_id=1, source_target_pairs={{0,16},{8,24},{16,32},{24,40},{32,48},{40,56},{48,64},{56,72},{64,... | collective-permute-start | bytes 2064392 | tf_op jit(solution)/shard_map/ppermute | solution.py:16
  172.9 1.7 copy-start.3
